TPU v7x, 128 devices: a whole 4x4x4 slice. The times are simulated.
128 devices in a mesh: rep: 8 (over z, y_lo), tp: 16 (over x, y_hi, core).
Axes of the slice: x: 4, y: 4 (y_hi: 2, y_lo: 2; y = y_hi * 2 + y_lo), z: 4, core: 2. Of those that a mesh axis runs over, the one named last changes fastest.
Arguments:
- exp_hidden: bfloat16 [512, 8192], P('rep', 'tp'), may hold values from -160 to 160
- exp_pre_gain: float32 [8192], P('tp'), may hold values from 0.25 to 1.75
- exp_gate: bfloat16 [8192, 28672], P('tp', 'rep'), may hold values from -0.0625 to 0.0625
- exp_up: bfloat16 [8192, 28672], P('tp', 'rep'), may hold values from -0.0625 to 0.0625
- exp_down: bfloat16 [28672, 8192], P('rep', 'tp'), may hold values from -0.03125 to 0.03125
- exp_out_gain: float32 [8192], P('tp'), may hold values from 0.25 to 1.75
- exp_head: bfloat16 [8192, 65536], P(None, ('rep', 'tp')), may hold values from -10 to 10
- ama_hidden: bfloat16 [512, 4096], P('rep', 'tp'), may hold values from -160 to 160
- ama_out_gain: float32 [4096], P('tp'), may hold values from 0.25 to 1.75
- ama_head: bfloat16 [4096, 65536], P(None, ('rep', 'tp')), may hold values from -10 to 10
- logit_scale: float32 [512], replicated, may hold values from 0.25 to 3
- prompt_of: int32 [512], replicated, may hold values from 0 to 15
- prior_picks: int32 [16, 24], replicated, may hold values from 0 to 65535
- valid_mask: int32 [65536], P(('rep', 'tp')), may hold values 0 or 1
Outputs:
- scores: float32 [512, 65536], P(None, ('rep', 'tp'))
- beam_best: float32 [512], replicated
All inputs are finite; a program needn't handle non-finite values. No bound on the sum of `valid_mask` on one device may be relied on, other than what follows from the above.
Results may differ from a plain program's by a relative error of at most 0.0034.
Values may be sent and summed in bfloat16 or wider, within the bound.
A program may use at most 128 MiB of HBM per device.

v0:
```python
import jax
import jax.numpy as jnp
from jax import lax
from jax.sharding import Mesh
from jax.sharding import PartitionSpec as P

DE = 8192
DA = 4096
TP = ("tp_0", "tp_1", "tp_2")
REP = ("rep_0", "rep_1")
REP_TP = ("rep_0", "rep_1", "tp_0", "tp_1", "tp_2")


norm_epsilon = 1e-05
contrast_weight = 0.5
hamming_weight = 0.7


def copy_for_each(array, axis):
    copies = jnp.broadcast_to(array, (lax.axis_size(axis), *array.shape))
    return lax.all_to_all(copies, axis, split_axis=0, concat_axis=0, tiled=True)


def of_everyone(array, axis):
    everything = copy_for_each(array, axis)
    return jnp.sum(everything, axis=0)


def in_order(blocks, dim):
    blocks = jnp.moveaxis(blocks, 0, dim)
    dims = blocks.shape
    return blocks.reshape(*dims[:dim], dims[dim] * dims[dim + 1], *dims[dim + 2 :])


def gather_directly(array, axis, dim):
    return in_order(copy_for_each(array, axis), dim)


def cut_along(array, dim, length):
    dims = array.shape
    blocks = array.reshape(*dims[:dim], length, dims[dim] // length, *dims[dim + 1 :])
    return jnp.moveaxis(blocks, dim, 0)


def sum_at_owner(array, axis, dim):
    length = lax.axis_size(axis)
    blocks = lax.all_to_all(cut_along(array, dim, length), axis, 0, 0, tiled=True)
    return jnp.sum(blocks, axis=0)


def together(arrays, axis):
    ends = [0]
    for a in arrays:
        ends.append(ends[-1] + a.size)
    subtotal = of_everyone(jnp.concatenate([a.ravel() for a in arrays]), axis)
    return tuple((subtotal[b:e].reshape(a.shape) for a, b, e in zip(arrays, ends, ends[1:])))


def gather_together(arrays, axis, dims):
    vector = jnp.concatenate([a.reshape(-1) for a in arrays])
    lines, at, done = (lax.all_gather(vector, axis), 0, [])
    for a, dim in zip(arrays, dims):
        blocks = lines[:, at : at + a.size].reshape(-1, *a.shape)
        done.append(in_order(blocks, dim))
        at += a.size
    return tuple(done)


def sent_together(arrays, axis, dim, along):
    widths = [a.shape[along] for a in arrays]
    both = jnp.concatenate(arrays, axis=along)
    filled = lax.all_gather(both, axis, axis=dim, tiled=True)
    return tuple(jnp.split(filled, [sum(widths[:k]) for k in range(1, len(widths))], axis=along))


def collected_together(array, axis):
    leaves = jax.tree.leaves(array)
    sequence = sorted(range(len(leaves)), key=lambda k: -leaves[k].size)
    width = (1, *leaves[sequence[0]].shape)[-1]
    lines = [
        jnp.pad(leaves[k].reshape(-1), (0, -leaves[k].size % width)).reshape(-1, width)
        for k in sequence
    ]
    both, at, found = (lax.all_gather(jnp.concatenate(lines), axis), 0, {})
    for k, line in zip(sequence, lines):
        piece = both[:, at : at + len(line)].reshape(len(both), -1)
        found[k] = piece[:, : leaves[k].size].reshape(-1, *leaves[k].shape)
        at += len(line)
    numbers = iter(range(len(leaves)))
    return jax.tree.map(lambda _: found[next(numbers)], array)


def combined_by_axis(array, axes, combine):
    for axis in axes:
        pieces = collected_together(array, axis)
        array = jax.tree.map(lambda part: part[0], pieces)
        for k in range(1, lax.axis_size(axis)):
            array = combine(array, jax.tree.map(lambda part: part[k], pieces))
    return array


def over_axes(array, axes):
    for axis in axes:
        array = lax.pmax(array, axis)
    return array


def scaled_rows(values, squares, width, gain):
    return (values * lax.rsqrt(squares[:, None] / width + norm_epsilon) * gain).astype(jnp.bfloat16)


def both_halves(rows_in, gate_weight, up_weight):
    gate = jnp.dot(rows_in, gate_weight, preferred_element_type=jnp.float32)
    up = jnp.dot(rows_in, up_weight, preferred_element_type=jnp.float32)
    return jnp.concatenate([gate, up], axis=1)


def gated_rows(summed, width):
    return (jax.nn.silu(summed[:, :width]) * summed[:, width:]).astype(jnp.bfloat16)


def merge_stats(first, second):
    top_exp = jnp.maximum(first[0], second[0])
    total_exp = first[1] * jnp.exp(first[0] - top_exp) + second[1] * jnp.exp(second[0] - top_exp)
    top_ama = jnp.maximum(first[2], second[2])
    total_ama = first[3] * jnp.exp(first[2] - top_ama) + second[3] * jnp.exp(second[2] - top_ama)
    return (top_exp, total_exp, top_ama, total_ama)


def body(
    exp_hidden,
    exp_pre_gain,
    exp_gate,
    exp_up,
    exp_down,
    exp_out_gain,
    exp_head,
    ama_hidden,
    ama_out_gain,
    ama_head,
    logit_scale,
    prompt_of,
    prior_picks,
    valid_mask,
):
    values_exp = exp_hidden.astype(jnp.float32)
    values_ama = ama_hidden.astype(jnp.float32)
    squares_exp = of_everyone(jnp.sum(values_exp * values_exp, axis=1), TP)
    normed_exp = scaled_rows(values_exp, squares_exp, DE, exp_pre_gain)
    rows_exp = gather_directly(normed_exp, REP, 0)
    width_exp = exp_gate.shape[1]
    summed_exp = lax.psum_scatter(
        both_halves(rows_exp, exp_gate, exp_up), TP, scatter_dimension=0, tiled=True
    )
    hidden_exp = gated_rows(summed_exp, width_exp)
    term_exp = jnp.dot(
        lax.all_gather(hidden_exp, TP, axis=0, tiled=True),
        exp_down,
        preferred_element_type=jnp.float32,
    )
    out_exp = sum_at_owner(term_exp, REP, 0)
    layer_exp = values_exp + out_exp
    final_sq_exp, final_sq_ama = together(
        (jnp.sum(layer_exp * layer_exp, axis=1), jnp.sum(values_ama * values_ama, axis=1)), TP
    )
    final_exp = scaled_rows(layer_exp, final_sq_exp, DE, exp_out_gain)
    final_ama = scaled_rows(values_ama, final_sq_ama, DA, ama_out_gain)
    features_exp, features_ama = gather_together((final_exp, final_ama), TP, (1, 1))
    full_exp, full_ama = sent_together((features_exp, features_ama), REP, 0, 1)
    logits_exp = logit_scale[:, None] * jnp.dot(
        full_exp, exp_head, preferred_element_type=jnp.float32
    )
    logits_ama = logit_scale[:, None] * jnp.dot(
        full_ama, ama_head, preferred_element_type=jnp.float32
    )
    local_top_exp = jnp.max(logits_exp, axis=1)
    local_top_ama = jnp.max(logits_ama, axis=1)
    local_exp = jnp.sum(jnp.exp(logits_exp - local_top_exp[:, None]), axis=1)
    local_ama = jnp.sum(jnp.exp(logits_ama - local_top_ama[:, None]), axis=1)
    top_exp, total_exp, top_ama, total_ama = combined_by_axis(
        (local_top_exp, local_exp, local_top_ama, local_ama), REP_TP, merge_stats
    )
    logp_exp = logits_exp - top_exp[:, None] - jnp.log(total_exp)[:, None]
    logp_ama = logits_ama - top_ama[:, None] - jnp.log(total_ama)[:, None]
    entries = exp_head.shape[1]
    first_entry = lax.axis_index(REP_TP) * entries
    vocab_ids = first_entry + jnp.arange(entries, dtype=jnp.int32)
    picks_row = jnp.take(prior_picks, prompt_of, axis=0)
    counts = jnp.sum(
        (picks_row[:, :, None] == vocab_ids[None, None, :]).astype(jnp.float32), axis=1
    )
    valid = valid_mask.astype(jnp.float32)[None, :]
    scores = logp_exp - contrast_weight * valid * logp_ama - hamming_weight * counts
    beam_best = over_axes(jnp.max(scores, axis=1), REP_TP)
    return (scores, beam_best)


def solution(mesh):
    torus = Mesh(mesh.devices.reshape(4, 2, 4, 2, 2), ("rep_0", "rep_1", "tp_0", "tp_1", "tp_2"))
    in_specs = (
        P(REP, TP),
        P(TP),
        P(TP, REP),
        P(TP, REP),
        P(REP, TP),
        P(TP),
        P(None, REP_TP),
        P(REP, TP),
        P(TP),
        P(None, REP_TP),
        P(),
        P(),
        P(),
        P(REP_TP),
    )
    out_specs = (P(None, REP_TP), P())
    return jax.shard_map(body, mesh=torus, in_specs=in_specs, out_specs=out_specs, check_vma=False)
```

profile of v0, /device:TPU:0, one launch (start us, length us, event | category | flops | bytes accessed | tf_op | source)
XLA Modules:
  0.0 663.6 jit_solution(17511272511628810336)
XLA Ops:
  7.2 0.0 copy-start
  7.2 0.0 reduce-scatter.2.cloned.1.call-start
  7.2 1.0 fusion.11
  8.2 14.5 %all_to_all.22 = f32[16,1,64]{2,1,0:T(1,128)S(1)} all-to-all(f32[16,1,64]{2,1,0:T(1,128)S(1)} %broadcast_in_dim.15), channel_id=1, replica_groups=mesh['rep_0'=4,'rep_1'=2,'tp_0'=4,'tp_1'=2,'tp_2'=2] {'tp_0','tp_1','tp_2'}, dimensions={0} | all-to-all | bytes 8192 | tf_op jit(solution)/shard_map/all_to_all | solution.py:21
  22.7 0.9 fusion.13
  23.7 15.4 %all_to_all.23 = bf16[8,64,512]{2,1,0:T(8,128)(2,1)S(1)} all-to-all(bf16[8,64,512]{2,1,0:T(8,128)(2,1)S(1)} %broadcast_in_dim.16), channel_id=1, replica_groups=mesh['rep_0'=4,'rep_1'=2,'tp_0'=4,'tp_1'=2,'tp_2'=2] {'rep_0','rep_1'}, dimensions={0} | all-to-all | bytes 1048576 | tf_op jit(solution)/shard_map/all_to_all | solution.py:21
  39.0 4.3 fusion.95
  43.3 2.1 fusion.96
  45.4 5.5 pad_maximum_fusion
  50.9 0.0 reduce-scatter.2.cloned.1.call-update
  50.9 0.0 all-gather.15.cloned.1.call-start
  51.0 128.2 %reduce-scatter.2.cloned.1.call-done = f32[32,7168]{1,0:T(8,128)} async-done(((f32[512,7168]{1,0:T(8,128)}), f32[32,7168]{1,0:T(8,128)}) %reduce-scatter.2.cloned.1.call-update) | async-done | bytes 917520 | tf_op jit(solution)/shard_map/reduce_scatter | solution.py:152
  179.1 2.0 fusion.10
  181.1 0.0 all-gather.15.cloned.1.call-update
  181.1 0.0 copy-start.3
  181.1 0.0 copy-start.2
  181.1 0.0 copy-start.5
  181.2 53.4 %all-gather.15.cloned.1.call-done = bf16[512,3584]{1,0:T(8,128)(2,1)} async-done(((bf16[32,3584]{1,0:T(8,128)(2,1)}), bf16[512,3584]{1,0:T(8,128)(2,1)}) %all-gather.15.cloned.1.call-update) | async-done | bytes 3670032 | tf_op jit(solution)/shard_map/all_gather | solution.py:157
  234.5 6.2 fusion.97
  240.7 4.4 all-to-all-start.2
  245.2 0.0 all-gather.19.cloned.1.call-start
  245.2 0.1 fusion.14
  245.3 16.0 %all-to-all-done.2 = f32[8,64,512]{2,1,0:T(8,128)S(1)} async-done(((f32[8,64,512]{2,1,0:T(8,128)}), f32[8,64,512]{2,1,0:T(8,128)S(1)}, u32[]{:S(2)}, u32[]{:S(2)}) %all-to-all-start.2) | async-done | bytes 1048608 | tf_op jit(solution)/shard_map/all_to_all | solution.py:47
  261.3 0.1 reduce_sum.83
  261.4 0.1 multiply_reduce_fusion
  261.5 0.1 pad_maximum_fusion.3
  261.6 12.5 %all_to_all.24 = f32[16,1,128]{2,1,0:T(1,128)S(1)} all-to-all(f32[16,1,128]{2,1,0:T(1,128)S(1)} %broadcast_in_dim.17), channel_id=1, replica_groups=mesh['rep_0'=4,'rep_1'=2,'tp_0'=4,'tp_1'=2,'tp_2'=2] {'tp_0','tp_1','tp_2'}, dimensions={0} | all-to-all | bytes 16384 | tf_op jit(solution)/shard_map/all_to_all | solution.py:21
  274.2 0.1 add_rsqrt_fusion.1
  274.3 0.1 fusion.17
  274.4 0.1 fusion.18
  274.5 0.6 pad_maximum_fusion.2
  275.2 0.0 all-gather.19.cloned.1.call-update
  275.2 0.2 all-gather.17.cloned.1.call-start
  275.4 41.4 %all-gather.19.cloned.1.call-done = bf16[786432]{0:T(1024)(128)(2,1)} async-done(((bf16[49152]{0:T(1024)(128)(2,1)}), bf16[786432]{0:T(1024)(128)(2,1)}) %all-gather.19.cloned.1.call-update) | async-done | bytes 1572880 | tf_op jit(solution)/shard_map/all_gather | solution.py:61
  316.8 1.8 reshape.1300
  318.6 0.1 slice.384
  318.8 0.3 copy.38
  319.1 0.1 copy.34
  319.2 0.1 copy.39
  319.4 1.3 pad_maximum_fusion.1
  320.7 0.0 all-gather.17.cloned.1.call-update
  320.7 1.0 gather_fusion
  321.8 0.1 broadcast_select_fusion
  322.0 9.4 %convert_reduce_fusion = f32[512,512]{1,0:T(8,128)S(1)} fusion(s32[512]{0:T(512)S(1)} %iota_add_fusion, s32[512,24]{1,0:T(8,128)S(1)} %broadcast_select_fusion), kind=kLoop, calls=%fused_computation.1 | loop fusion | flops 18612224 | bytes 1099776 | tf_op jit(solution)/shard_map/reduce_sum | solution.py:189
  331.4 0.3 copy.32
  331.7 234.9 %all-gather.17.cloned.1.call-done = bf16[512,12288]{1,0:T(8,128)(2,1)} async-done(((bf16[64,12288]{1,0:T(8,128)(2,1)}), bf16[512,12288]{1,0:T(8,128)(2,1)}) %all-gather.17.cloned.1.call-update) | async-done | bytes 12582928 | tf_op jit(solution)/shard_map/all_gather | solution.py:72
  566.6 10.9 %fusion.94 = (f32[512]{0:T(512)S(1)}, f32[512,512]{0,1:T(8,128)S(1)}) fusion(bf16[8192,512]{1,0:T(8,128)(2,1)} %param.20, bf16[512,12288]{1,0:T(8,128)(2,1)} %all-gather.17.cloned.1.call-done, f32[512]{0:T(512)S(1)} %copy-done.8), kind=kOutput, calls=%fused_computation.163 | convolution fusion | flops 4295491072 | bytes 17829888 | tf_op jit(solution)/shard_map/dot_general | solution.py:170
  577.5 0.2 exponential_reduce_fusion.1
  577.7 5.9 fusion.93
  583.6 0.2 exponential_reduce_fusion
  583.8 12.4 %all-gather.6 = f32[4,4,512]{2,1,0:T(4,128)S(1)} all-gather(f32[1,4,512]{2,1,0:T(4,128)S(1)} %maximum_bitcast_fusion), channel_id=3, replica_groups=mesh['rep_0'=4,'rep_1'=2,'tp_0'=4,'tp_1'=2,'tp_2'=2] {'rep_0'}, dimensions={0}, use_global_device_ids=true | all-gather | bytes 40960 | tf_op jit(solution)/shard_map/all_gather | solution.py:84
  596.2 0.1 fusion.59
  596.3 4.4 all-gather.7
  600.7 12.2 %all-gather.8 = f32[4,4,512]{2,1,0:T(4,128)S(1)} all-gather(f32[1,4,512]{2,1,0:T(4,128)S(1)} %maximum_bitcast_fusion.2), channel_id=5, replica_groups=mesh['rep_0'=4,'rep_1'=2,'tp_0'=4,'tp_1'=2,'tp_2'=2] {'tp_0'}, dimensions={0}, use_global_device_ids=true | all-gather | bytes 40960 | tf_op jit(solution)/shard_map/all_gather | solution.py:84
  612.9 0.1 fusion.35
  613.0 5.9 all-gather.9
  618.9 1.8 all-gather.10
  620.8 0.4 fusion.83
  621.2 1.3 copy.33
  622.5 10.2 %pmax.35 = f32[512]{0:T(512)S(1)} all-reduce(f32[512]{0:T(512)S(1)} %get-tuple-element.14), channel_id=1, replica_groups=mesh['rep_0'=4,'rep_1'=2,'tp_0'=4,'tp_1'=2,'tp_2'=2] {'rep_0'}, use_global_device_ids=true, to_apply=%region_13.14 | all-reduce | flops 512 | bytes 4096 | tf_op jit(solution)/shard_map/pmax | solution.py:104
  632.6 4.9 pmax.36
  637.5 10.1 %pmax.37 = f32[512]{0:T(512)S(1)} all-reduce(f32[512]{0:T(512)S(1)} %pmax.36), channel_id=1, replica_groups=mesh['rep_0'=4,'rep_1'=2,'tp_0'=4,'tp_1'=2,'tp_2'=2] {'tp_0'}, use_global_device_ids=true, to_apply=%region_15.16 | all-reduce | flops 512 | bytes 4096 | tf_op jit(solution)/shard_map/pmax | solution.py:104
  647.6 6.4 pmax.38
  654.1 3.0 pmax.39
  (38 shorter events, 0.4 us)
Async XLA Ops:
  7.2 313.6 %copy-start = (s32[16,24]{1,0:T(8,128)S(1)}, s32[16,24]{1,0:T(8,128)}, u32[]{:S(2)}) copy-start(s32[16,24]{1,0:T(8,128)} %param.26) | copy-start | bytes 4612
  7.2 171.9 %reduce-scatter.2.cloned.1.call-start = ((), (), s32[]{:S(2)}) async-start(), calls=%async_computation.5 | async-start | bytes 15597568 | tf_op jit(solution)/shard_map/reduce_scatter | solution.py:152
  39.0 4.3 copy-start.1
  50.9 183.6 %all-gather.15.cloned.1.call-start = ((), (), s32[]{:S(2)}) async-start(), calls=%async_computation.6 | async-start | bytes 3899392 | tf_op jit(solution)/shard_map/all_gather | solution.py:157
  181.1 64.1 %copy-start.3 = (bf16[64,256]{1,0:T(8,128)(2,1)S(1)}, bf16[64,256]{1,0:T(8,128)(2,1)}, u32[]{:S(2)}) copy-start(bf16[64,256]{1,0:T(8,128)(2,1)} %param.21) | copy-start | bytes 98308
  181.1 80.3 %copy-start.2 = (bf16[64,512]{1,0:T(8,128)(2,1)S(1)}, bf16[64,512]{1,0:T(8,128)(2,1)}, u32[]{:S(2)}) copy-start(bf16[64,512]{1,0:T(8,128)(2,1)} %param.14) | copy-start | bytes 196612
  181.1 93.1 %copy-start.5 = (f32[512]{0:T(512)S(1)}, f32[512]{0:T(512)}, u32[]{:S(2)}) copy-start(f32[512]{0:T(512)} %param.19) | copy-start | bytes 6148
  181.1 93.3 %copy-start.7 = (f32[256]{0:T(256)S(1)}, f32[256]{0:T(256)}, u32[]{:S(2)}) copy-start(f32[256]{0:T(256)} %param.22) | copy-start | bytes 3076
  240.7 20.6 %all-to-all-start.2 = ((f32[8,64,512]{2,1,0:T(8,128)}), f32[8,64,512]{2,1,0:T(8,128)S(1)}, u32[]{:S(2)}, u32[]{:S(2)}) async-start(f32[8,64,512]{2,1,0:T(8,128)} %bitcast.2), calls=%async_computation.3 | async-start | bytes 2097152 | tf_op jit(solution)/shard_map/all_to_all | solution.py:47
  245.2 71.7 %all-gather.19.cloned.1.call-start = ((), (), s32[]{:S(2)}) async-start(), calls=%async_computation.8 | async-start | bytes 1671168 | tf_op jit(solution)/shard_map/all_gather | solution.py:61
  275.2 291.4 %all-gather.17.cloned.1.call-start = ((), (), s32[]{:S(2)}) async-start(), calls=%async_computation.7 | async-start | bytes 14155776 | tf_op jit(solution)/shard_map/all_gather | solution.py:72
  319.1 1.6 copy-start.4
  320.7 11.1 %copy-start.6 = (s32[512]{0:T(512)S(1)}, s32[512]{0:T(512)}, u32[]{:S(2)}) copy-start(s32[512]{0:T(512)} %param.27) | copy-start | bytes 6148
  320.7 246.0 %copy-start.8 = (f32[512]{0:T(512)S(1)}, f32[512]{0:T(512)}, u32[]{:S(2)}) copy-start(f32[512]{0:T(512)} %param.24) | copy-start | bytes 6148
Sparse Core Ops, SparseCore 0:
  51.0 128.0 reduce-scatter.1
  182.4 52.0 all-gather.14
  275.3 41.4 all-gather.18
  320.8 245.7 all-gather.16
where the time goes:
time: 665 us; the launch traced here: 664 us
  waiting for transfers between devices  474 us (71%)
  blocking collectives  114 us (17%)
  matrix products  29.2 us (4%)
  other arithmetic  22.6 us (3%)
  between operations  14.2 us (2%)
    all_gather x1, waiting for transfers between devices, sent_together(): filled = lax.all_gather(both, axis, axis=dim, tiled=True)  235 us
    reduce_scatter x1, waiting for transfers between devices, body(): lax.psum_scatter(both_halves(rows_exp, exp_gate, exp_up), TP, scatter_dim...  128 us
    all_gather x1, waiting for transfers between devices, body(): lax.all_gather(hidden_exp, TP, axis=0, tiled=True)  53.4 us
    all_to_all x3, blocking collectives, copy_for_each(): return lax.all_to_all(copies, axis, split_axis=0, concat_axis=0, tiled=True)  42.4 us
    all_gather x1, waiting for transfers between devices, gather_together(): lines, at, done = (lax.all_gather(vector, axis), 0, [])  41.4 us
    all_gather x5, blocking collectives, collected_together(): both, at, found = (lax.all_gather(jnp.concatenate(lines), axis), 0, {})  36.7 us
    pmax x5, blocking collectives, over_axes(): array = lax.pmax(array, axis)  34.6 us
    all_to_all x1, waiting for transfers between devices, sum_at_owner(): lax.all_to_all(cut_along(array, dim, length), axis, 0, 0, tiled=True)  16 us
  transfers between devices with their start and end apart: 5, of which 5 were waited for; matrix products, arithmetic and copies ran while one was open for 2% of the time, Pallas kernels for 0%

commit v1 on v0

v1 whole, which is shorter than its diff:
```python
import functools

import jax
import jax.numpy as jnp
from jax import lax
from jax.experimental import pallas as pl
from jax.experimental.pallas import tpu as pltpu
from jax.sharding import Mesh
from jax.sharding import PartitionSpec as P

DE = 8192
DA = 4096
AXES = ("z", "l", "x", "h", "c")
REP = ("z", "l")
TP = ("x", "h", "c")
ALL = REP + TP

norm_epsilon = 1e-05
contrast_weight = 0.5
hamming_weight = 0.7
LOWEST = -3.0e38

ROWS = 512
BLOCK = 64
KDIM = 512
HALF = 1792
CHUNK = 256
CHUNKS = HALF // CHUNK
KAMA = 256
WIDE = 512
BF16 = jnp.bfloat16
F32 = jnp.float32

XH = [(d // 2, d % 2) for d in range(1, 8)]
TPO = [(d // 4, (d // 2) % 2, d % 2) for d in range(1, 16)]
ZL = [(d // 2, d % 2) for d in range(1, 8)]


def dot(a, b):
    return jnp.dot(a, b, preferred_element_type=F32)


def eye128():
    return lax.broadcasted_iota(jnp.int32, (128, 128), 0) == lax.broadcasted_iota(
        jnp.int32, (128, 128), 1
    )


def to_row(column):
    return jnp.sum(jnp.where(eye128(), jnp.broadcast_to(column, (128, 128)), 0.0), 0, keepdims=True)


def to_column(row):
    return jnp.sum(jnp.where(eye128(), jnp.broadcast_to(row, (128, 128)), 0.0), 1, keepdims=True)


def aligned(v, m):
    return pl.multiple_of(v, m)


def kernel(
    hid_in, pre_gain, gate, up, down, out_gain, head, ama_in, ama_gain, ahead,
    lscale, prompt, picks, valid,
    scores, best,
    XR, XG, W, DOWN, HEAD, AHEAD, PB, RR, HID, ACC, OB, OR, FE, FA, AIN, LE, LA,
    STS, ST, TOT, RC, SFS, SF, SGS, SG, RE, RA, CNT, SBUF, PG, OG, AG,
    s_loc, s_wl, s_ws, s_wr, s_xs, s_xr, s_bs, s_br, s_sts, s_str,
    s_rs, s_rr, s_hs, s_hr, s_cs, s_cr, s_os, s_or, s_rings, s_ringr, s_fs, s_fr,
    s_sfs, s_sfr, s_sgs, s_sgr, s_qs, s_qr,
):
    z, l, x, h, c = (lax.axis_index(a) for a in AXES)
    sib = 1 - c
    r = z * 2 + l
    b = x * 2 + h
    t = x * 4 + h * 2 + c
    y = h * 2 + l

    def remote(src, dst, ss, rs, **where):
        return pltpu.make_async_remote_copy(
            src_ref=src, dst_ref=dst, send_sem=ss, recv_sem=rs,
            device_id=where, device_id_type=pl.DeviceIdType.MESH,
        )

    sends = []

    def send(src, dst, ss, rs, **where):
        cp = remote(src, dst, ss, rs, **where)
        cp.start()
        sends.append(cp)

    def recv(dst, rs):
        remote(dst, dst, rs, rs, c=sib).wait_recv()

    def local(src, dst, sem):
        return pltpu.make_async_copy(src, dst, sem)

    def zl(d, sign):
        dz, dl = ZL[d]
        return lax.rem(z + sign * dz + 4, 4), lax.rem(l + dl, 2)

    def xh(d, sign):
        dx, dh = XH[d]
        return lax.rem(x + sign * dx + 4, 4), lax.rem(h + dh, 2)

    def tp(d, sign):
        dx, dh, dc = TPO[d]
        return lax.rem(x + sign * dx + 4, 4), lax.rem(h + dh, 2), lax.rem(c + dc, 2)

    def wcols(half, j):
        return pl.ds(aligned(half * HALF + j * CHUNK, 128), CHUNK)

    def wlocal(j, i, ref):
        return local(ref.at[:, wcols(c, j)], W.at[j, c, :, pl.ds(i * CHUNK, CHUNK)], s_wl.at[j, i])

    first = [
        local(hid_in, XR.at[r], s_loc.at[0]),
        local(pre_gain, PG, s_loc.at[1]),
        local(ama_in, AIN, s_loc.at[2]),
        local(ama_gain, AG, s_loc.at[3]),
        local(out_gain, OG, s_loc.at[4]),
    ]
    for cp in first:
        cp.start()
    for j in range(CHUNKS):
        wlocal(j, 0, gate).start()
        wlocal(j, 1, up).start()
    late = [
        local(down, DOWN, s_loc.at[5]),
        local(ahead, AHEAD, s_loc.at[6]),
        local(head, HEAD, s_loc.at[7]),
    ]

    barrier = pltpu.get_barrier_semaphore()

    def greet(**where):
        pl.semaphore_signal(barrier, inc=1, device_id=where, device_id_type=pl.DeviceIdType.MESH)

    for d in range(7):
        pz, q = zl(d, 1)
        greet(z=pz, l=q)
    for d in range(15):
        px, ph, pc = tp(d, 1)
        greet(x=px, h=ph, c=pc)
    greet(h=1 - h, l=1 - l)
    pl.semaphore_wait(barrier, 23)

    for d in range(7):
        pz, q = zl(d, 1)
        send(hid_in, XR.at[r], s_xs.at[d], s_xr.at[d], z=pz, l=q)
    for j in range(CHUNKS):
        for i, ref in enumerate((gate, up)):
            send(
                ref.at[:, wcols(sib, j)], W.at[j, c, :, pl.ds(i * CHUNK, CHUNK)],
                s_ws.at[j, i], s_wr.at[j, i], c=sib,
            )

    def ring(index, sets, places, me):
        prv, nxt = lax.rem(me + 3, 4), lax.rem(me + 1, 4)
        opp = lax.rem(me + 2, 4)
        lo, hi = pl.ds(0, 32), pl.ds(32, 32)
        full = pl.ds(0, 64)

        def start():
            mine = sets(me, full)
            send(mine, mine, s_rings.at[index, 0], s_ringr.at[index, 0], **places(nxt))
            send(mine, mine, s_rings.at[index, 1], s_ringr.at[index, 1], **places(prv))

        def pass_next():
            recv(sets(prv, full), s_ringr.at[index, 0])
            part = sets(prv, lo)
            send(part, part, s_rings.at[index, 2], s_ringr.at[index, 2], **places(nxt))

        def pass_prev():
            recv(sets(nxt, full), s_ringr.at[index, 1])
            part = sets(nxt, hi)
            send(part, part, s_rings.at[index, 3], s_ringr.at[index, 3], **places(prv))

        def finish():
            recv(sets(opp, lo), s_ringr.at[index, 2])
            recv(sets(opp, hi), s_ringr.at[index, 3])

        return start, pass_next, pass_prev, finish, (me, prv, nxt, opp)

    def y_place(p):
        return dict(h=p // 2, l=lax.rem(p, 2))

    every4, every2 = pl.ds(0, 4), pl.ds(0, 2)

    def rings_x_y_z(ref, cols, first_index):
        a = ring(first_index, lambda p, k: ref.at[p, h, c, z, l, k, cols], lambda p: dict(x=p), x)
        bb = ring(
            first_index + 1,
            lambda p, k: ref.at[every4, p // 2, c, z, lax.rem(p, 2), k, cols], y_place, y,
        )
        d = ring(
            first_index + 2,
            lambda p, k: ref.at[every4, every2, c, p, every2, k, cols], lambda p: dict(z=p), z,
        )
        return a, bb, d

    def rings_z_y_x(ref, cols, first_index):
        a = ring(first_index, lambda p, k: ref.at[x, h, c, p, l, k, cols], lambda p: dict(z=p), z)
        bb = ring(
            first_index + 1,
            lambda p, k: ref.at[x, p // 2, c, every4, lax.rem(p, 2), k, cols], y_place, y,
        )
        d = ring(
            first_index + 2,
            lambda p, k: ref.at[p, every2, c, every4, every2, k, cols], lambda p: dict(x=p), x,
        )
        return a, bb, d

    for cp in first:
        cp.wait()
    values_a = AIN[...].astype(F32)
    squares_a = jnp.sum(values_a * values_a, axis=1, keepdims=True)
    FA[x, h, c, z, l] = (values_a * AG[...]).astype(BF16)
    ama = rings_x_y_z(FA, pl.ds(0, KAMA), 0)
    ama[0][0]()

    def take_rows(rr, d):
        XG[c, rr] = (XR[rr].astype(F32) * PG[...]).astype(BF16)
        send(XG.at[c, rr], XG.at[c, rr], s_bs.at[d], s_br.at[d], c=sib)

    take_rows(r, 7)
    for cp in late:
        cp.start()
    for d in range(7):
        pz, q = zl(d, -1)
        rr = pz * 2 + q
        recv(XR.at[rr], s_xr.at[d])
        take_rows(rr, d)

    for q in range(4):
        v = XR[pl.ds(2 * q, 2)].reshape(128, KDIM).astype(F32)
        STS[q : q + 1, :] = to_row(jnp.sum(v * v, axis=1, keepdims=True))
    for d in range(15):
        px, ph, pc = tp(d, 1)
        send(STS, ST.at[d], s_sts.at[d], s_str.at[d], x=px, h=ph, c=pc)

    ama[0][1]()
    ama[0][2]()

    for d in range(7):
        pz, q = zl(d, -1)
        recv(XG.at[sib, pz * 2 + q], s_br.at[d])
    recv(XG.at[sib, r], s_br.at[7])

    def rs_copy(j, d):
        px, ph = xh(d, 1)
        rows = pl.ds(aligned((px * 2 + ph) * BLOCK, BLOCK), BLOCK)
        return remote(PB.at[j, rows, :], RR.at[j, d], s_rs.at[j, d], s_rr.at[j, d], x=px, h=ph)

    def products(j, _):
        for i, ref in enumerate((gate, up)):
            wlocal(j, i, ref).wait()
            recv(W.at[j, sib, :, pl.ds(i * CHUNK, CHUNK)], s_wr.at[j, i])

        def block(q, _):
            rows = pl.ds(aligned(q * 128, 128), 128)
            pair = pl.ds(q * 2, 2)
            p = dot(XG[0, pair].reshape(128, KDIM), W[j, 0])
            p += dot(XG[1, pair].reshape(128, KDIM), W[j, 1])
            PB[j, rows, :] = p.astype(BF16)
            return 0

        lax.fori_loop(0, 4, block, 0)
        for d in range(7):
            rs_copy(j, d).start()
        return 0

    lax.fori_loop(0, CHUNKS, products, 0)

    ama[0][3]()
    ama[1][0]()

    for d in range(15):
        recv(ST.at[d], s_str.at[d])
    tot = STS[...]
    for d in range(15):
        tot += ST[d]
    TOT[...] = tot
    col = to_column(TOT[pl.ds(x, 1), :])
    RC[...] = jnp.broadcast_to(lax.rsqrt(col / DE + norm_epsilon), (128, 128))
    factor = RC[pl.ds(aligned(h * BLOCK, BLOCK), BLOCK), :][:, 0:1]

    ids = t * WIDE + r * (16 * WIDE) + lax.broadcasted_iota(jnp.int32, (16, WIDE), 1)
    per_prompt = jnp.zeros((16, WIDE), F32)
    for k in range(24):
        per_prompt += (picks[:, k : k + 1] == ids).astype(F32)
    chosen = (lax.broadcasted_iota(jnp.int32, (16, ROWS), 0) == prompt[...]).astype(F32)
    CNT[...] = lax.dot_general(
        chosen.astype(BF16), per_prompt.astype(BF16), (((0,), (0,)), ((), ())),
        preferred_element_type=F32,
    )

    ama[1][1]()
    ama[1][2]()

    own_rows = pl.ds(aligned(b * BLOCK, BLOCK), BLOCK)

    def hid_copy(j, d):
        px, ph = xh(d, 1)
        piece = HID.at[c, j, own_rows, :]
        return remote(piece, piece, s_hs.at[j, d], s_hr.at[j, d], x=px, h=ph)

    def hidden(j, _):
        for d in range(7):
            recv(RR.at[j, d], s_rr.at[j, d])
        both = PB[j, own_rows, :].astype(F32)
        for d in range(7):
            both += RR[j, d].astype(F32)
        g = both[:, :CHUNK] * factor
        u = both[:, CHUNK:] * factor
        HID[c, j, own_rows, :] = (g / (1.0 + jnp.exp(-g)) * u).astype(BF16)
        for d in range(7):
            hid_copy(j, d).start()
        return 0

    lax.fori_loop(0, 3, hidden, 0)
    ama[1][3]()
    ama[2][0]()
    lax.fori_loop(3, CHUNKS, hidden, 0)
    ama[2][1]()
    ama[2][2]()

    late[0].wait()
    ACC[...] = jnp.zeros_like(ACC)

    def core_copy(j):
        return remote(HID.at[c, j], HID.at[c, j], s_cs.at[j], s_cr.at[j], c=sib)

    def gathered(j, _):
        for d in range(7):
            px, ph = xh(d, -1)
            rows = pl.ds(aligned((px * 2 + ph) * BLOCK, BLOCK), BLOCK)
            recv(HID.at[c, j, rows, :], s_hr.at[j, d])
        core_copy(j).start()

        def block(q, _):
            rows = pl.ds(aligned(q * 128, 128), 128)
            depth = pl.ds(aligned(c * HALF + j * CHUNK, CHUNK), CHUNK)
            ACC[rows, :] += dot(HID[c, j, rows, :], DOWN[depth, :])
            return 0

        lax.fori_loop(0, 4, block, 0)
        return 0

    def from_core(j, _):
        recv(HID.at[sib, j], s_cr.at[j])

        def block(q, _):
            rows = pl.ds(aligned(q * 128, 128), 128)
            depth = pl.ds(aligned(sib * HALF + j * CHUNK, CHUNK), CHUNK)
            ACC[rows, :] += dot(HID[sib, j, rows, :], DOWN[depth, :])
            return 0

        lax.fori_loop(0, 4, block, 0)
        return 0

    def step(j, _):
        gathered(j, 0)
        from_core(j - 1, 0)
        return 0

    gathered(0, 0)
    lax.fori_loop(1, CHUNKS, step, 0)
    from_core(CHUNKS - 1, 0)

    for q in range(8):
        OB[q] = ACC[q * BLOCK : (q + 1) * BLOCK, :].astype(BF16)
    for d in range(7):
        pz, q = zl(d, 1)
        send(OB.at[pz * 2 + q], OR.at[d], s_os.at[d], s_or.at[d], z=pz, l=q)
    layer = XR[r].astype(F32) + ACC[pl.ds(aligned(r * BLOCK, BLOCK), BLOCK), :]
    for d in range(7):
        recv(OR.at[d], s_or.at[d])
        layer += OR[d].astype(F32)
    FE[x, h, c, z, l] = (layer * OG[...]).astype(BF16)

    low, high = pl.ds(0, 256), pl.ds(256, 256)
    one = rings_x_y_z(FE, low, 3)
    two = rings_z_y_x(FE, high, 6)
    one[0][0]()
    two[0][0]()

    squares = jnp.concatenate([jnp.sum(layer * layer, axis=1, keepdims=True), squares_a], axis=0)
    SFS[...] = jnp.broadcast_to(to_row(squares), (8, 128))
    for d in range(15):
        px, ph, pc = tp(d, 1)
        send(SFS, SF.at[t], s_sfs.at[d], s_sfr.at[d], x=px, h=ph, c=pc)

    for g in (one[0], two[0]):
        g[1]()
        g[2]()
    for g, n in ((one[0], one[1]), (two[0], two[1])):
        g[3]()
        n[0]()

    def totals():
        SF[t] = SFS[...]
        for d in range(15):
            px, ph, pc = tp(d, -1)
            recv(SF.at[px * 4 + ph * 2 + pc], s_sfr.at[d])
        total = SF[0]
        for d in range(1, 16):
            total += SF[d]
        SGS[...] = total
        for d in range(7):
            pz, q = zl(d, 1)
            send(SGS, SG.at[r], s_sgs.at[d], s_sgr.at[d], z=pz, l=q)

    for g in (one[1], two[1]):
        g[1]()
        g[2]()
    totals()

    def over(ref, cols, index, n):
        def go(where):
            send(where, where, s_fs.at[index, n], s_fr.at[index, n], c=sib)
        return go

    def a_set(ref, cc, p, cols):
        return ref.at[every4, every2, cc, p, every2, pl.ds(0, 64), cols]

    def b_set(ref, cc, p, cols):
        return ref.at[p, every2, cc, every4, every2, pl.ds(0, 64), cols]

    def to_core(ref, maker, p, cols, index, n):
        s = maker(ref, c, p, cols)
        send(s, s, s_fs.at[index, n], s_fr.at[index, n], c=sib)

    def from_other(ref, maker, p, cols, index, n):
        recv(maker(ref, sib, p, cols), s_fr.at[index, n])

    one[1][3]()
    one[2][0]()
    two[1][3]()
    two[2][0]()

    ama_cols = pl.ds(0, KAMA)
    ama[2][3]()
    a_places = ama[2][4]
    for n in range(4):
        to_core(FA, a_set, a_places[n], ama_cols, 0, n)
    to_core(FE, a_set, z, low, 1, 0)
    to_core(FE, b_set, x, high, 2, 0)

    late[1].wait()
    late[2].wait()
    for n in range(4):
        from_other(FA, a_set, a_places[n], ama_cols, 0, n)

    def ama_block(q, _):
        def one_t(k, acc):
            xx, hh, cc = k // 4, lax.rem(k // 2, 2), lax.rem(k, 2)
            v = FA[xx, hh, cc, q].reshape(128, KAMA)
            return acc + dot(v, AHEAD[pl.ds(aligned(k * KAMA, KAMA), KAMA), :])

        rows = pl.ds(aligned(q * 128, 128), 128)
        LA[rows, :] = lax.fori_loop(0, 16, one_t, jnp.zeros((128, WIDE), F32))
        return 0

    lax.fori_loop(0, 4, ama_block, 0)

    LE[...] = jnp.zeros_like(LE)

    def use_a(p):
        def one_t(k, acc):
            xx, hh, cc = k // 4, lax.rem(k // 2, 2), lax.rem(k, 2)
            v = FE[xx, hh, cc, p, :, :, 0:256].reshape(128, 256)
            return acc + dot(v, HEAD[pl.ds(aligned(k * KDIM, KDIM), 256), :])

        rows = pl.ds(aligned(p * 128, 128), 128)
        LE[rows, :] += lax.fori_loop(0, 16, one_t, jnp.zeros((128, WIDE), F32))

    def use_b(p):
        def block(q, _):
            def one_t(k, acc):
                hh, cc = k // 2, lax.rem(k, 2)
                v = FE[p, hh, cc, q, :, :, 256:512].reshape(128, 256)
                first_row = (p * 4 + k) * KDIM + 256
                return acc + dot(v, HEAD[pl.ds(aligned(first_row, 256), 256), :])

            rows = pl.ds(aligned(q * 128, 128), 128)
            LE[rows, :] += lax.fori_loop(0, 4, one_t, jnp.zeros((128, WIDE), F32))
            return 0

        lax.fori_loop(0, 4, block, 0)

    za, xb = one[2][4], two[2][4]
    one[2][1]()
    to_core(FE, a_set, za[1], low, 1, 1)
    two[2][1]()
    to_core(FE, b_set, xb[1], high, 2, 1)
    one[2][2]()
    to_core(FE, a_set, za[2], low, 1, 2)
    two[2][2]()
    to_core(FE, b_set, xb[2], high, 2, 2)
    for n in range(3):
        from_other(FE, a_set, za[n], low, 1, n)
        use_a(za[n])
        from_other(FE, b_set, xb[n], high, 2, n)
        use_b(xb[n])

    SG[r] = SGS[...]
    for d in range(7):
        pz, q = zl(d, -1)
        recv(SG.at[pz * 2 + q], s_sgr.at[d])
    for q in range(4):
        ls = to_column(lscale[q : q + 1, :])
        for n in range(2):
            col = to_column(SG[2 * q + n, 0:1, :])
            k = n * BLOCK
            rows = slice(q * 128 + k, q * 128 + k + BLOCK)
            fe = lax.rsqrt(col[:BLOCK] / DE + norm_epsilon) * ls[k : k + BLOCK]
            fa = lax.rsqrt(col[BLOCK:] / DA + norm_epsilon) * ls[k : k + BLOCK]
            RE[rows, :] = jnp.broadcast_to(fe, (BLOCK, 128))
            RA[rows, :] = jnp.broadcast_to(fa, (BLOCK, 128))

    one[2][3]()
    to_core(FE, a_set, za[3], low, 1, 3)
    two[2][3]()
    to_core(FE, b_set, xb[3], high, 2, 3)
    from_other(FE, a_set, za[3], low, 1, 3)
    use_a(za[3])
    from_other(FE, b_set, xb[3], high, 2, 3)
    use_b(xb[3])

    vmask = valid[...].astype(F32)
    half_valid = contrast_weight * vmask
    for q in range(4):
        rows = slice(q * 128, (q + 1) * 128)
        le = LE[rows, :] * RE[rows, 0:1]
        la = LA[rows, :] * RA[rows, 0:1]
        LE[rows, :] = le
        LA[rows, :] = la
        me = jnp.max(le, axis=1, keepdims=True)
        ma = jnp.max(la, axis=1, keepdims=True)
        se = jnp.sum(jnp.exp(le - me), axis=1, keepdims=True)
        sa = jnp.sum(jnp.exp(la - ma), axis=1, keepdims=True)
        raw = le - half_valid * la - hamming_weight * CNT[rows, :]
        used = jnp.broadcast_to(vmask, raw.shape) > 0.5
        m1 = jnp.max(jnp.where(used, raw, LOWEST), axis=1, keepdims=True)
        m0 = jnp.max(jnp.where(used, LOWEST, raw), axis=1, keepdims=True)
        lines = [to_row(v) for v in (me, se, ma, sa, m1, m0, me, me)]
        SBUF[0, c, :, rows] = jnp.concatenate(lines, axis=0)

    def merge(parts):
        me = functools.reduce(jnp.maximum, [p[0:1] for p in parts])
        ma = functools.reduce(jnp.maximum, [p[2:3] for p in parts])
        se = sum(p[1:2] * jnp.exp(p[0:1] - me) for p in parts)
        sa = sum(p[3:4] * jnp.exp(p[2:3] - ma) for p in parts)
        m1 = functools.reduce(jnp.maximum, [p[4:5] for p in parts])
        m0 = functools.reduce(jnp.maximum, [p[5:6] for p in parts])
        return jnp.concatenate([me, se, ma, sa, m1, m0, me, me], axis=0)

    mine = SBUF.at[0, c]
    send(mine, mine, s_qs.at[0, 0], s_qr.at[0, 0], c=sib)
    recv(SBUF.at[0, sib], s_qr.at[0, 0])
    merged = merge([SBUF[0, 0], SBUF[0, 1]])
    for phase, (me, place) in enumerate(
        ((x, lambda p: dict(x=p)), (y, y_place), (z, lambda p: dict(z=p))), start=1
    ):
        SBUF[phase, me] = merged
        mine = SBUF.at[phase, me]
        for d in range(1, 4):
            send(mine, mine, s_qs.at[phase, d], s_qr.at[phase, d], **place(lax.rem(me + d, 4)))
        for d in range(1, 4):
            recv(SBUF.at[phase, lax.rem(me + 4 - d, 4)], s_qr.at[phase, d])
        merged = merge([SBUF[phase, k] for k in range(4)])

    le_all = jnp.log(merged[1:2])
    la_all = jnp.log(merged[3:4])
    shift_e = merged[0:1] + le_all
    shift_a = merged[2:3] + la_all
    best[...] = jnp.maximum(
        merged[4:5] - shift_e + contrast_weight * shift_a, merged[5:6] - shift_e
    )
    for q in range(4):
        rows = slice(q * 128, (q + 1) * 128)
        ce, ca = to_column(merged[0:1, rows]), to_column(merged[2:3, rows])
        de, da = to_column(le_all[:, rows]), to_column(la_all[:, rows])
        pe = LE[rows, :] - ce - de
        pa = LA[rows, :] - ca - da
        scores[rows, :] = pe - half_valid * pa - hamming_weight * CNT[rows, :]

    for cp in sends:
        cp.wait_send()

    def drain(j, _):
        for d in range(7):
            rs_copy(j, d).wait_send()
            hid_copy(j, d).wait_send()
        core_copy(j).wait_send()
        return 0

    lax.fori_loop(0, CHUNKS, drain, 0)


def body(
    exp_hidden, exp_pre_gain, exp_gate, exp_up, exp_down, exp_out_gain, exp_head,
    ama_hidden, ama_out_gain, ama_head, logit_scale, prompt_of, prior_picks, valid_mask,
):
    hbm = pl.BlockSpec(memory_space=pl.ANY)
    vmem = pl.BlockSpec(memory_space=pltpu.VMEM)
    dma = pltpu.SemaphoreType.DMA
    scratch = [
        pltpu.VMEM((8, BLOCK, KDIM), BF16),
        pltpu.VMEM((2, 8, BLOCK, KDIM), BF16),
        pltpu.VMEM((CHUNKS, 2, KDIM, 2 * CHUNK), BF16),
        pltpu.VMEM((2 * HALF, KDIM), BF16),
        pltpu.VMEM((DE, WIDE), BF16),
        pltpu.VMEM((DA, WIDE), BF16),
        pltpu.VMEM((CHUNKS, ROWS, 2 * CHUNK), BF16),
        pltpu.VMEM((CHUNKS, 7, BLOCK, 2 * CHUNK), BF16),
        pltpu.VMEM((2, CHUNKS, ROWS, CHUNK), BF16),
        pltpu.VMEM((ROWS, KDIM), F32),
        pltpu.VMEM((8, BLOCK, KDIM), BF16),
        pltpu.VMEM((7, BLOCK, KDIM), BF16),
        pltpu.VMEM((4, 2, 2, 4, 2, BLOCK, KDIM), BF16),
        pltpu.VMEM((4, 2, 2, 4, 2, BLOCK, KAMA), BF16),
        pltpu.VMEM((BLOCK, KAMA), BF16),
        pltpu.VMEM((ROWS, WIDE), F32),
        pltpu.VMEM((ROWS, WIDE), F32),
        pltpu.VMEM((8, 128), F32),
        pltpu.VMEM((15, 8, 128), F32),
        pltpu.VMEM((8, 128), F32),
        pltpu.VMEM((128, 128), F32),
        pltpu.VMEM((8, 128), F32),
        pltpu.VMEM((16, 8, 128), F32),
        pltpu.VMEM((8, 128), F32),
        pltpu.VMEM((8, 8, 128), F32),
        pltpu.VMEM((ROWS, 128), F32),
        pltpu.VMEM((ROWS, 128), F32),
        pltpu.VMEM((ROWS, WIDE), F32),
        pltpu.VMEM((4, 4, 8, ROWS), F32),
        pltpu.VMEM((1, KDIM), F32),
        pltpu.VMEM((1, KDIM), F32),
        pltpu.VMEM((1, KAMA), F32),
        dma((8,)), dma((CHUNKS, 2)), dma((CHUNKS, 2)), dma((CHUNKS, 2)),
        dma((7,)), dma((7,)), dma((8,)), dma((8,)), dma((15,)), dma((15,)),
        dma((CHUNKS, 7)), dma((CHUNKS, 7)), dma((CHUNKS, 7)), dma((CHUNKS, 7)),
        dma((CHUNKS,)), dma((CHUNKS,)), dma((7,)), dma((7,)),
        dma((9, 4)), dma((9, 4)), dma((3, 4)), dma((3, 4)),
        dma((15,)), dma((15,)), dma((7,)), dma((7,)), dma((4, 4)), dma((4, 4)),
    ]
    scores, best = pl.pallas_call(
        kernel,
        out_shape=(
            jax.ShapeDtypeStruct((ROWS, WIDE), F32),
            jax.ShapeDtypeStruct((1, ROWS), F32),
        ),
        in_specs=[hbm] * 10 + [vmem] * 4,
        out_specs=(vmem, vmem),
        scratch_shapes=scratch,
        compiler_params=pltpu.CompilerParams(
            collective_id=0, has_side_effects=True, vmem_limit_bytes=63 * 1024 * 1024
        ),
        cost_estimate=pl.CostEstimate(
            flops=12_000_000_000, bytes_accessed=25_000_000, transcendentals=600_000
        ),
    )(
        exp_hidden, exp_pre_gain.reshape(1, KDIM), exp_gate, exp_up, exp_down,
        exp_out_gain.reshape(1, KDIM), exp_head, ama_hidden, ama_out_gain.reshape(1, KAMA),
        ama_head, logit_scale.reshape(4, 128), prompt_of.reshape(1, ROWS), prior_picks,
        valid_mask.reshape(1, WIDE),
    )
    return scores, best.reshape(ROWS)


def solution(mesh):
    torus = Mesh(mesh.devices.reshape(4, 2, 4, 2, 2), AXES)
    in_specs = (
        P(REP, TP), P(TP), P(TP, REP), P(TP, REP), P(REP, TP), P(TP), P(None, ALL),
        P(REP, TP), P(TP), P(None, ALL), P(), P(), P(), P(ALL),
    )
    out_specs = (P(None, ALL), P())
    return jax.shard_map(body, mesh=torus, in_specs=in_specs, out_specs=out_specs, check_vma=False)
```

time: 665 us -> 210 us (0.32)
  waiting for transfers between devices: 474 us -> 0 us
  Pallas kernels: 0 us -> 205 us
  blocking collectives: 114 us -> 0 us
  matrix products: 29.2 us -> 0 us
  other arithmetic: 22.6 us -> 0 us
  between operations: 14.2 us -> 0.64 us
    all_gather x3 -> x0, waiting for transfers between devices: 330 us -> none  [the longest x1 235 us: sent_together(): filled = lax.all_gather(both, axis, axis=dim, tiled=True)]
    pallas_call x0 -> x1, Pallas kernels: none -> 205 us  [body(): pl.pallas_call(kernel, out_shape=(jax.ShapeDtypeStruct((ROWS, WIDE), F32)...]
    reduce_scatter x1 -> x0, waiting for transfers between devices: 128 us -> none  [body(): lax.psum_scatter(both_halves(rows_exp, exp_gate, exp_up), TP, scatter_dim...]
    all_to_all x3 -> x0, blocking collectives: 42.4 us -> none  [copy_for_each(): return lax.all_to_all(copies, axis, split_axis=0, concat_axis=0, tiled=True)]
    all_gather x5 -> x0, blocking collectives: 36.7 us -> none  [collected_together(): both, at, found = (lax.all_gather(jnp.concatenate(lines), axis), 0, {})]
    pmax x5 -> x0, blocking collectives: 34.6 us -> none  [over_axes(): array = lax.pmax(array, axis)]
    dot_general x5 -> x0, matrix products: 29.2 us -> none  [the longest x1 10.9 us: body(): jnp.dot(full_exp, exp_head, preferred_element_type=jnp.float32)]
    all_to_all x1 -> x0, waiting for transfers between devices: 16 us -> none  [sum_at_owner(): lax.all_to_all(cut_along(array, dim, length), axis, 0, 0, tiled=True)]
  transfers between devices with their start and end apart: 5 -> 0, of which waited for: 5 -> 0; matrix products, arithmetic and copies ran while one was open for 2% -> 0% of each run, Pallas kernels for 0% -> 0%
where the time goes in v1:
time: 210 us; the launch traced here: 209 us
  Pallas kernels  205 us (98%)
  local copies, waits for them, and re-layouts  3.52 us (2%)
    pallas_call x1, Pallas kernels, body(): pl.pallas_call(kernel, out_shape=(jax.ShapeDtypeStruct((ROWS, WIDE), F32)...  205 us

profile of v1, /device:TPU:0, one launch (start us, length us, event | category | flops | bytes accessed | tf_op | source)
XLA Modules:
  0.0 209.4 jit_solution(7170976767183680733)
XLA Ops:
  0.6 205.2 %shard_map.149 = (f32[512,512]{1,0:T(8,128)}, f32[1,512]{1,0:T(1,128)}) custom-call(bf16[64,512]{1,0:T(8,128)(2,1)} %hid_in.1, f32[1,512]{1,0:T(1,128)} %bitcast.8, bf16[512,3584]{1,0:T(8,128)(2,1)} %gate.1, bf16[512,3584]{1,0:T(8,128)(2,1)} %up.1, bf16[3584,512]{1,0:T(8,128)(2,1)} %down.1, f32[1,512]{1,0:T(1,128)} %bitcast.9, bf16[8192,512]{1,0:T(8,128)(2,1)} %head.1, ...), custom_call_target="tpu_custom_call" | custom-call | flops 12000000000 | bytes 25000000 | tf_op jit(solution)/shard_map/pallas_call | solution.py:648
  205.9 2.3 %copy.18 = f32[512,512]{1,0:T(8,128)} copy(f32[512,512]{1,0:T(8,128)} %get-tuple-element.8) | data formatting | bytes 2097152
  208.1 1.3 copy.19

commit v2 on v1

v2 whole, which is shorter than its diff:
```python
import functools

import jax
import jax.numpy as jnp
from jax import lax
from jax.experimental import pallas as pl
from jax.experimental.pallas import tpu as pltpu
from jax.sharding import Mesh
from jax.sharding import PartitionSpec as P

DE = 8192
DA = 4096
AXES = ("z", "l", "x", "h", "c")
REP = ("z", "l")
TP = ("x", "h", "c")
ALL = REP + TP

norm_epsilon = 1e-05
contrast_weight = 0.5
hamming_weight = 0.7
LOWEST = -3.0e38

ROWS = 512
BLOCK = 64
KDIM = 512
HALF = 1792
CHUNK = 256
CHUNKS = HALF // CHUNK
KAMA = 256
WIDE = 512
BF16 = jnp.bfloat16
F32 = jnp.float32

XH = [(d // 2, d % 2) for d in range(1, 8)]
TPO = [(d // 4, (d // 2) % 2, d % 2) for d in range(1, 16)]
ZL = [(d // 2, d % 2) for d in range(1, 8)]


def dot(a, b):
    return jnp.dot(a, b, preferred_element_type=F32)


def eye128():
    return lax.broadcasted_iota(jnp.int32, (128, 128), 0) == lax.broadcasted_iota(
        jnp.int32, (128, 128), 1
    )


def to_row(column):
    return jnp.sum(jnp.where(eye128(), jnp.broadcast_to(column, (128, 128)), 0.0), 0, keepdims=True)


def to_column(row):
    return jnp.sum(jnp.where(eye128(), jnp.broadcast_to(row, (128, 128)), 0.0), 1, keepdims=True)


def aligned(v, m):
    return pl.multiple_of(v, m)


def kernel(
    hid_in, pre_gain, gate, up, down, out_gain, head, ama_in, ama_gain, ahead,
    lscale, prompt, picks, valid,
    raw_out, stats_out,
    XR, XG, W, DOWN, HEADA, HEADB, AHEAD, PB, RR, HID, ACC, OB, OR, FE, FA, AIN, LE, LA,
    STS, ST, FS, FR, SFS, SF, SGS, SG, RE, CNT, SBUF, PG, OG, AG,
    s_loc, s_wl, s_ws, s_wr, s_xs, s_xr, s_bs, s_br, s_sts, s_str, s_frs, s_frr,
    s_rs, s_rr, s_hs, s_hr, s_cs, s_cr, s_os, s_or, s_rings, s_ringr, s_fs, s_fr,
    s_sfs, s_sfr, s_sgs, s_sgr, s_qs, s_qr, s_out,
):
    z, l, x, h, c = (lax.axis_index(a) for a in AXES)
    sib = 1 - c
    r = z * 2 + l
    b = x * 2 + h
    t = x * 4 + h * 2 + c
    y = h * 2 + l

    def remote(src, dst, ss, rs, **where):
        return pltpu.make_async_remote_copy(
            src_ref=src, dst_ref=dst, send_sem=ss, recv_sem=rs,
            device_id=where, device_id_type=pl.DeviceIdType.MESH,
        )

    sends = []

    def send(src, dst, ss, rs, **where):
        cp = remote(src, dst, ss, rs, **where)
        cp.start()
        sends.append(cp)

    def recv(dst, rs):
        remote(dst, dst, rs, rs, c=sib).wait_recv()

    def local(src, dst, sem):
        return pltpu.make_async_copy(src, dst, sem)

    def zl(d, sign):
        dz, dl = ZL[d]
        return lax.rem(z + sign * dz + 4, 4), lax.rem(l + dl, 2)

    def xh(d, sign):
        dx, dh = XH[d]
        return lax.rem(x + sign * dx + 4, 4), lax.rem(h + dh, 2)

    def tp(d, sign):
        dx, dh, dc = TPO[d]
        return lax.rem(x + sign * dx + 4, 4), lax.rem(h + dh, 2), lax.rem(c + dc, 2)

    def wcols(half, j):
        return pl.ds(aligned(half * HALF + j * CHUNK, 128), CHUNK)

    def wpart(j, core, i):
        rows = pl.ds(aligned(core * KDIM, KDIM), KDIM)
        return W.at[j, rows, pl.ds(i * CHUNK, CHUNK)]

    def wlocal(j, i, ref):
        return local(ref.at[:, wcols(c, j)], wpart(j, c, i), s_wl.at[j, i])

    first = [
        local(hid_in, XR.at[r], s_loc.at[0]),
        local(pre_gain, PG, s_loc.at[1]),
        local(ama_in, AIN, s_loc.at[2]),
        local(ama_gain, AG, s_loc.at[3]),
        local(out_gain, OG, s_loc.at[4]),
    ]
    for cp in first:
        cp.start()
    for j in range(CHUNKS):
        wlocal(j, 0, gate).start()
        wlocal(j, 1, up).start()
    late = [
        local(down, DOWN, s_loc.at[5]),
        local(ahead, AHEAD, s_loc.at[6]),
        local(head.at[:, pl.ds(0, 256), :], HEADA, s_loc.at[7]),
        local(head.at[:, pl.ds(256, 256), :], HEADB, s_loc.at[8]),
    ]

    barrier = pltpu.get_barrier_semaphore()

    def greet(**where):
        pl.semaphore_signal(barrier, inc=1, device_id=where, device_id_type=pl.DeviceIdType.MESH)

    for d in range(7):
        pz, q = zl(d, 1)
        greet(z=pz, l=q)
    for d in range(15):
        px, ph, pc = tp(d, 1)
        greet(x=px, h=ph, c=pc)
    greet(h=1 - h, l=1 - l)
    pl.semaphore_wait(barrier, 23)

    for d in range(7):
        pz, q = zl(d, 1)
        send(hid_in, XR.at[r], s_xs.at[d], s_xr.at[d], z=pz, l=q)
    for j in range(CHUNKS):
        for i, ref in enumerate((gate, up)):
            send(
                ref.at[:, wcols(sib, j)], wpart(j, c, i),
                s_ws.at[j, i], s_wr.at[j, i], c=sib,
            )

    def ring(index, sets, places, me):
        prv, nxt = lax.rem(me + 3, 4), lax.rem(me + 1, 4)
        opp = lax.rem(me + 2, 4)
        lo, hi = pl.ds(0, 32), pl.ds(32, 32)
        full = pl.ds(0, 64)

        def start():
            mine = sets(me, full)
            send(mine, mine, s_rings.at[index, 0], s_ringr.at[index, 0], **places(nxt))
            send(mine, mine, s_rings.at[index, 1], s_ringr.at[index, 1], **places(prv))

        def pass_next():
            recv(sets(prv, full), s_ringr.at[index, 0])
            part = sets(prv, lo)
            send(part, part, s_rings.at[index, 2], s_ringr.at[index, 2], **places(nxt))

        def pass_prev():
            recv(sets(nxt, full), s_ringr.at[index, 1])
            part = sets(nxt, hi)
            send(part, part, s_rings.at[index, 3], s_ringr.at[index, 3], **places(prv))

        def finish():
            recv(sets(opp, lo), s_ringr.at[index, 2])
            recv(sets(opp, hi), s_ringr.at[index, 3])

        return start, pass_next, pass_prev, finish, (me, prv, nxt, opp)

    def y_place(p):
        return dict(h=p // 2, l=lax.rem(p, 2))

    every4, every2 = pl.ds(0, 4), pl.ds(0, 2)

    def rings_x_y_z(ref, cols, first_index, split=False):
        a = ring(first_index, lambda p, k: ref.at[p, h, c, z, l, k, cols], lambda p: dict(x=p), x)
        bb = ring(
            first_index + 1,
            lambda p, k: ref.at[every4, p // 2, c, z, lax.rem(p, 2), k, cols], y_place, y,
        )
        if split:
            def d(yy, n):
                return ring(
                    first_index + 6 + n,
                    lambda p, k: ref.at[every4, yy // 2, c, p, lax.rem(yy, 2), k, cols],
                    lambda p: dict(z=p), z,
                )
        else:
            d = ring(
                first_index + 2,
                lambda p, k: ref.at[every4, every2, c, p, every2, k, cols], lambda p: dict(z=p), z,
            )
        return a, bb, d

    def rings_z_y_x(ref, cols, first_index):
        a = ring(first_index, lambda p, k: ref.at[x, h, c, p, l, k, cols], lambda p: dict(z=p), z)
        bb = ring(
            first_index + 1,
            lambda p, k: ref.at[x, p // 2, c, every4, lax.rem(p, 2), k, cols], y_place, y,
        )

        def d(yy, n):
            return ring(
                first_index + 6 + n,
                lambda p, k: ref.at[p, yy // 2, c, every4, lax.rem(yy, 2), k, cols],
                lambda p: dict(x=p), x,
            )

        return a, bb, d

    def a_set(ref, cc, p, cols):
        return ref.at[every4, every2, cc, p, every2, pl.ds(0, 64), cols]

    def b_set(ref, cc, p, cols):
        return ref.at[p, every2, cc, every4, every2, pl.ds(0, 64), cols]

    def to_core(ref, maker, p, cols, index, n):
        s = maker(ref, c, p, cols)
        send(s, s, s_fs.at[index, n], s_fr.at[index, n], c=sib)

    def from_other(ref, maker, p, cols, index, n):
        recv(maker(ref, sib, p, cols), s_fr.at[index, n])

    for cp in first:
        cp.wait()
    values_x = XR[r].astype(F32)
    values_a = AIN[...].astype(F32)
    squares = jnp.concatenate(
        [jnp.sum(v * v, axis=1, keepdims=True) for v in (values_x, values_a)], axis=0
    )
    STS[...] = jnp.broadcast_to(to_row(squares), (8, 128))
    for d in range(15):
        px, ph, pc = tp(d, 1)
        send(STS, ST.at[d], s_sts.at[d], s_str.at[0], x=px, h=ph, c=pc)
    recv(ST, s_str.at[0])
    total = STS[...]
    for d in range(15):
        total += ST[d]
    lane = lax.broadcasted_iota(jnp.int32, (8, 128), 1)
    means = jnp.where(lane < BLOCK, total / DE, total / DA)
    FS[...] = lax.rsqrt(means + norm_epsilon)
    for d in range(7):
        pz, q = zl(d, 1)
        send(FS, FR.at[d], s_frs.at[d], s_frr.at[0], z=pz, l=q)
    own_factors = to_column(FS[0:1, :])

    FA[x, h, c, z, l] = (values_a * own_factors[BLOCK:] * AG[...]).astype(BF16)
    ama = rings_x_y_z(FA, pl.ds(0, KAMA), 0)
    ama[0][0]()

    def take_rows(rr, d, factors):
        XG[c, rr] = (XR[rr].astype(F32) * factors[:BLOCK] * PG[...]).astype(BF16)
        send(XG.at[c, rr], XG.at[c, rr], s_bs.at[d], s_br.at[d], c=sib)

    take_rows(r, 7, own_factors)
    for cp in late:
        cp.start()
    recv(FR, s_frr.at[0])
    for d in range(7):
        pz, q = zl(d, -1)
        rr = pz * 2 + q
        recv(XR.at[rr], s_xr.at[d])
        take_rows(rr, d, to_column(FR[d, 0:1, :]))

    ama[0][1]()
    ama[0][2]()

    for d in range(7):
        pz, q = zl(d, -1)
        recv(XG.at[sib, pz * 2 + q], s_br.at[d])
    recv(XG.at[sib, r], s_br.at[7])

    def rs_copy(j, d):
        px, ph = xh(d, 1)
        rows = pl.ds(aligned((px * 2 + ph) * BLOCK, BLOCK), BLOCK)
        return remote(PB.at[j, rows, :], RR.at[j, d], s_rs.at[j], s_rr.at[j], x=px, h=ph)

    def products(j, _):
        for i, ref in enumerate((gate, up)):
            wlocal(j, i, ref).wait()
            recv(wpart(j, sib, i), s_wr.at[j, i])

        def block(q, _):
            rows = pl.ds(aligned(q * 256, 256), 256)
            quad = pl.ds(q * 4, 4)
            lhs = jnp.concatenate([XG[k, quad].reshape(256, KDIM) for k in range(2)], axis=1)
            PB[j, rows, :] = dot(lhs, W[j]).astype(BF16)
            return 0

        lax.fori_loop(0, 2, block, 0)
        for d in range(7):
            rs_copy(j, d).start()
        return 0

    lax.fori_loop(0, CHUNKS, products, 0)

    ama[0][3]()
    ama[1][0]()

    ids = t * WIDE + r * (16 * WIDE) + lax.broadcasted_iota(jnp.int32, (16, WIDE), 1)
    per_prompt = jnp.zeros((16, WIDE), F32)
    for k in range(24):
        per_prompt += (picks[:, k : k + 1] == ids).astype(F32)
    chosen = (lax.broadcasted_iota(jnp.int32, (16, ROWS), 0) == prompt[...]).astype(F32)
    CNT[...] = lax.dot_general(
        chosen.astype(BF16), per_prompt.astype(BF16), (((0,), (0,)), ((), ())),
        preferred_element_type=F32,
    )

    ama[1][1]()
    ama[1][2]()
    ama[1][3]()
    ama[2][0]()

    own_rows = pl.ds(aligned(b * BLOCK, BLOCK), BLOCK)

    def hid_copy(j, d):
        px, ph = xh(d, 1)
        piece = HID.at[c, j, own_rows, :]
        return remote(piece, piece, s_hs.at[j], s_hr.at[j], x=px, h=ph)

    def hidden(j, _):
        recv(RR.at[j], s_rr.at[j])
        both = PB[j, own_rows, :].astype(F32)
        for d in range(7):
            both += RR[j, d].astype(F32)
        g = both[:, :CHUNK]
        u = both[:, CHUNK:]
        HID[c, j, own_rows, :] = (g / (1.0 + jnp.exp(-g)) * u).astype(BF16)
        for d in range(7):
            hid_copy(j, d).start()
        return 0

    lax.fori_loop(0, 3, hidden, 0)
    ama[2][1]()
    ama[2][2]()
    lax.fori_loop(3, 5, hidden, 0)
    ama[2][3]()
    a_places = ama[2][4]
    ama_cols = pl.ds(0, KAMA)
    for n in range(4):
        to_core(FA, a_set, a_places[n], ama_cols, 0, n)
    lax.fori_loop(5, CHUNKS, hidden, 0)

    late[1].wait()
    for n in range(4):
        from_other(FA, a_set, a_places[n], ama_cols, 0, n)

    def ama_block(q, _):
        rows = pl.ds(aligned(q * 256, 256), 256)
        LA[rows, :] = jnp.zeros((256, WIDE), F32)

        def part(k, _):
            lhs = jnp.concatenate(
                [FA[k, n // 2, n % 2, pl.ds(q * 2, 2)].reshape(256, KAMA) for n in range(4)], axis=1
            )
            LA[rows, :] += dot(lhs, AHEAD[pl.ds(aligned(k * 4 * KAMA, 4 * KAMA), 4 * KAMA), :])
            return 0

        lax.fori_loop(0, 4, part, 0)
        return 0

    lax.fori_loop(0, 2, ama_block, 0)

    late[0].wait()
    ACC[...] = jnp.zeros_like(ACC)

    def core_copy(j):
        return remote(HID.at[c, j], HID.at[c, j], s_cs.at[j], s_cr.at[j], c=sib)

    def gathered(j, _):
        recv(HID.at[c, j, pl.ds(0, 7 * BLOCK), :], s_hr.at[j])
        core_copy(j).start()

        def block(q, _):
            rows = pl.ds(aligned(q * 256, 256), 256)
            depth = pl.ds(aligned(c * HALF + j * CHUNK, CHUNK), CHUNK)
            ACC[rows, :] += dot(HID[c, j, rows, :], DOWN[depth, :])
            return 0

        lax.fori_loop(0, 2, block, 0)
        return 0

    def from_core(j, _):
        recv(HID.at[sib, j], s_cr.at[j])

        def block(q, _):
            rows = pl.ds(aligned(q * 256, 256), 256)
            depth = pl.ds(aligned(sib * HALF + j * CHUNK, CHUNK), CHUNK)
            ACC[rows, :] += dot(HID[sib, j, rows, :], DOWN[depth, :])
            return 0

        lax.fori_loop(0, 2, block, 0)
        return 0

    def step(j, _):
        gathered(j, 0)
        from_core(j - 1, 0)
        return 0

    gathered(0, 0)
    lax.fori_loop(1, CHUNKS, step, 0)
    from_core(CHUNKS - 1, 0)

    for q in range(8):
        OB[q] = ACC[q * BLOCK : (q + 1) * BLOCK, :].astype(BF16)
    for d in range(7):
        pz, q = zl(d, 1)
        send(OB.at[pz * 2 + q], OR.at[d], s_os.at[d], s_or.at[0], z=pz, l=q)
    layer = values_x + ACC[pl.ds(aligned(r * BLOCK, BLOCK), BLOCK), :]
    recv(OR, s_or.at[0])
    for d in range(7):
        layer += OR[d].astype(F32)
    FE[x, h, c, z, l] = (layer * OG[...]).astype(BF16)

    low, high = pl.ds(0, 256), pl.ds(256, 256)
    one = rings_x_y_z(FE, low, 3, split=True)
    two = rings_z_y_x(FE, high, 7)
    one[0][0]()
    two[0][0]()

    squares = jnp.sum(layer * layer, axis=1, keepdims=True)
    squares = jnp.concatenate([squares, squares], axis=0)
    SFS[...] = jnp.broadcast_to(to_row(squares), (8, 128))
    for d in range(15):
        px, ph, pc = tp(d, 1)
        send(SFS, SF.at[d], s_sfs.at[d], s_sfr.at[0], x=px, h=ph, c=pc)

    for g in (one[0], two[0]):
        g[1]()
        g[2]()
    y_order = one[1][4]
    last_one = [one[2](p, n) for n, p in enumerate(y_order)]
    last_two = [two[2](p, n) for n, p in enumerate(y_order)]
    for g, n, e in ((one[0], one[1], last_one), (two[0], two[1], last_two)):
        g[3]()
        n[0]()
        e[0][0]()
    for k in (1, 2):
        for n, e in ((one[1], last_one), (two[1], last_two)):
            n[k]()
            e[k][0]()

    recv(SF, s_sfr.at[0])
    total = SFS[...]
    for d in range(15):
        total += SF[d]
    SGS[...] = total
    for d in range(7):
        pz, q = zl(d, 1)
        send(SGS, SG.at[d], s_sgs.at[d], s_sgr.at[0], z=pz, l=q)

    for n, e in ((one[1], last_one), (two[1], last_two)):
        n[3]()
        e[3][0]()
    to_core(FE, a_set, z, low, 1, 0)
    to_core(FE, b_set, x, high, 2, 0)
    late[2].wait()
    late[3].wait()
    LE[...] = jnp.zeros_like(LE)

    def use_a(p):
        def part(k, _):
            lhs = jnp.concatenate(
                [FE[k, n // 2, n % 2, p, :, :, 0:256].reshape(128, 256) for n in range(4)], axis=1
            )
            rows = pl.ds(aligned(p * 128, 128), 128)
            LE[rows, :] += dot(lhs, HEADA[pl.ds(k * 4, 4)].reshape(1024, WIDE))
            return 0

        lax.fori_loop(0, 4, part, 0)

    def use_b(p):
        def part(q, _):
            pair = pl.ds(q * 2, 2)
            lhs = jnp.concatenate(
                [FE[p, n // 2, n % 2, pair, :, :, 256:512].reshape(256, 256) for n in range(4)], axis=1
            )
            rows = pl.ds(aligned(q * 256, 256), 256)
            LE[rows, :] += dot(lhs, HEADB[pl.ds(p * 4, 4)].reshape(1024, WIDE))
            return 0

        lax.fori_loop(0, 2, part, 0)

    za, xb = last_one[0][4], last_two[0][4]
    for n in range(4):
        for e in (last_one, last_two):
            e[n][1]()
            e[n][2]()
    for n in (1, 2):
        to_core(FE, a_set, za[n], low, 1, n)
        to_core(FE, b_set, xb[n], high, 2, n)
    for n in range(3):
        from_other(FE, a_set, za[n], low, 1, n)
        use_a(za[n])
        from_other(FE, b_set, xb[n], high, 2, n)
        use_b(xb[n])

    recv(SG, s_sgr.at[0])
    for q in range(4):
        ls = to_column(lscale[q : q + 1, :])
        RE[1, pl.ds(q * 128, 128), :] = jnp.broadcast_to(ls, (128, 128))

    def row_factors(rr, line):
        rows = pl.ds(aligned(rr * BLOCK, BLOCK), BLOCK)
        col = lax.rsqrt(to_column(line)[:BLOCK] / DE + norm_epsilon)
        RE[0, rows, :] = col * RE[1, rows, :]

    row_factors(r, SGS[0:1, :])
    for d in range(7):
        pz, q = zl(d, -1)
        row_factors(pz * 2 + q, SG[d, 0:1, :])

    for n in range(4):
        for e in (last_one, last_two):
            e[n][3]()
    to_core(FE, a_set, za[3], low, 1, 3)
    to_core(FE, b_set, xb[3], high, 2, 3)
    from_other(FE, a_set, za[3], low, 1, 3)
    use_a(za[3])
    from_other(FE, b_set, xb[3], high, 2, 3)
    use_b(xb[3])

    vmask = valid[...].astype(F32)
    half_valid = contrast_weight * vmask
    for q in range(4):
        rows = pl.ds(q * 128, 128)
        le = LE[rows, :] * RE[0, rows, 0:1]
        la = LA[rows, :] * RE[1, rows, 0:1]
        me = jnp.max(le, axis=1, keepdims=True)
        ma = jnp.max(la, axis=1, keepdims=True)
        se = jnp.sum(jnp.exp(le - me), axis=1, keepdims=True)
        sa = jnp.sum(jnp.exp(la - ma), axis=1, keepdims=True)
        raw = le - half_valid * la - hamming_weight * CNT[rows, :]
        LE[rows, :] = raw
        local(LE.at[rows], raw_out.at[rows], s_out.at[q]).start()
        used = jnp.broadcast_to(vmask, raw.shape) > 0.5
        m1 = jnp.max(jnp.where(used, raw, LOWEST), axis=1, keepdims=True)
        m0 = jnp.max(jnp.where(used, LOWEST, raw), axis=1, keepdims=True)
        lines = [to_row(v) for v in (me, se, ma, sa, m1, m0, me, me)]
        SBUF[0, c, :, rows] = jnp.concatenate(lines, axis=0)

    def merge(parts):
        me = functools.reduce(jnp.maximum, [p[0:1] for p in parts])
        ma = functools.reduce(jnp.maximum, [p[2:3] for p in parts])
        se = sum(p[1:2] * jnp.exp(p[0:1] - me) for p in parts)
        sa = sum(p[3:4] * jnp.exp(p[2:3] - ma) for p in parts)
        m1 = functools.reduce(jnp.maximum, [p[4:5] for p in parts])
        m0 = functools.reduce(jnp.maximum, [p[5:6] for p in parts])
        return jnp.concatenate([me, se, ma, sa, m1, m0, me, me], axis=0)

    mine = SBUF.at[0, c]
    send(mine, mine, s_qs.at[0, 0], s_qr.at[0, 0], c=sib)
    recv(SBUF.at[0, sib], s_qr.at[0, 0])
    merged = merge([SBUF[0, 0], SBUF[0, 1]])
    for phase, (me, place) in enumerate(
        ((x, lambda p: dict(x=p)), (y, y_place), (z, lambda p: dict(z=p))), start=1
    ):
        SBUF[phase, me] = merged
        mine = SBUF.at[phase, me]
        for d in range(1, 4):
            send(mine, mine, s_qs.at[phase, d], s_qr.at[phase, d], **place(lax.rem(me + d, 4)))
        for d in range(1, 4):
            recv(SBUF.at[phase, lax.rem(me + 4 - d, 4)], s_qr.at[phase, d])
        merged = merge([SBUF[phase, k] for k in range(4)])

    stats_out[...] = merged
    for q in range(4):
        rows = pl.ds(q * 128, 128)
        local(LE.at[rows], raw_out.at[rows], s_out.at[q]).wait()

    for cp in sends:
        cp.wait_send()

    def drain(j, _):
        sent = RR.at[j]
        remote(sent, sent, s_rs.at[j], s_rr.at[j], c=sib).wait_send()
        sent = HID.at[c, j, pl.ds(0, 7 * BLOCK), :]
        remote(sent, sent, s_hs.at[j], s_hr.at[j], c=sib).wait_send()
        core_copy(j).wait_send()
        return 0

    lax.fori_loop(0, CHUNKS, drain, 0)


def finish(raw, stats, valid, scores, best):
    shift_e = stats[0:1, :] + jnp.log(stats[1:2, :])
    shift_a = stats[2:3, :] + jnp.log(stats[3:4, :])
    best[...] = jnp.maximum(
        stats[4:5, :] - shift_e + contrast_weight * shift_a, stats[5:6, :] - shift_e
    )
    half_valid = contrast_weight * valid[...].astype(F32)
    for q in range(4):
        rows = slice(q * 128, (q + 1) * 128)
        back = half_valid * to_column(shift_a[:, rows]) - to_column(shift_e[:, rows])
        scores[rows, :] = raw[rows, :] + back


def body(
    exp_hidden, exp_pre_gain, exp_gate, exp_up, exp_down, exp_out_gain, exp_head,
    ama_hidden, ama_out_gain, ama_head, logit_scale, prompt_of, prior_picks, valid_mask,
):
    hbm = pl.BlockSpec(memory_space=pl.ANY)
    vmem = pl.BlockSpec(memory_space=pltpu.VMEM)
    dma = pltpu.SemaphoreType.DMA
    scratch = [
        pltpu.VMEM((8, BLOCK, KDIM), BF16),
        pltpu.VMEM((2, 8, BLOCK, KDIM), BF16),
        pltpu.VMEM((CHUNKS, 2 * KDIM, 2 * CHUNK), BF16),
        pltpu.VMEM((2 * HALF, KDIM), BF16),
        pltpu.VMEM((16, 256, WIDE), BF16),
        pltpu.VMEM((16, 256, WIDE), BF16),
        pltpu.VMEM((DA, WIDE), BF16),
        pltpu.VMEM((CHUNKS, ROWS, 2 * CHUNK), BF16),
        pltpu.VMEM((CHUNKS, 7, BLOCK, 2 * CHUNK), BF16),
        pltpu.VMEM((2, CHUNKS, ROWS, CHUNK), BF16),
        pltpu.VMEM((ROWS, KDIM), F32),
        pltpu.VMEM((8, BLOCK, KDIM), BF16),
        pltpu.VMEM((7, BLOCK, KDIM), BF16),
        pltpu.VMEM((4, 2, 2, 4, 2, BLOCK, KDIM), BF16),
        pltpu.VMEM((4, 2, 2, 4, 2, BLOCK, KAMA), BF16),
        pltpu.VMEM((BLOCK, KAMA), BF16),
        pltpu.VMEM((ROWS, WIDE), F32),
        pltpu.VMEM((ROWS, WIDE), F32),
        pltpu.VMEM((8, 128), F32),
        pltpu.VMEM((15, 8, 128), F32),
        pltpu.VMEM((8, 128), F32),
        pltpu.VMEM((7, 8, 128), F32),
        pltpu.VMEM((8, 128), F32),
        pltpu.VMEM((15, 8, 128), F32),
        pltpu.VMEM((8, 128), F32),
        pltpu.VMEM((7, 8, 128), F32),
        pltpu.VMEM((2, ROWS, 128), F32),
        pltpu.VMEM((ROWS, WIDE), F32),
        pltpu.VMEM((4, 4, 8, ROWS), F32),
        pltpu.VMEM((1, KDIM), F32),
        pltpu.VMEM((1, KDIM), F32),
        pltpu.VMEM((1, KAMA), F32),
        dma((9,)), dma((CHUNKS, 2)), dma((CHUNKS, 2)), dma((CHUNKS, 2)),
        dma((7,)), dma((7,)), dma((8,)), dma((8,)), dma((15,)), dma((1,)), dma((7,)), dma((1,)),
        dma((CHUNKS,)), dma((CHUNKS,)), dma((CHUNKS,)), dma((CHUNKS,)),
        dma((CHUNKS,)), dma((CHUNKS,)), dma((7,)), dma((1,)),
        dma((17, 4)), dma((17, 4)), dma((3, 4)), dma((3, 4)),
        dma((15,)), dma((1,)), dma((7,)), dma((1,)), dma((4, 4)), dma((4, 4)), dma((4,)),
    ]
    raw, stats = pl.pallas_call(
        kernel,
        out_shape=(
            jax.ShapeDtypeStruct((ROWS, WIDE), F32),
            jax.ShapeDtypeStruct((8, ROWS), F32),
        ),
        in_specs=[hbm] * 10 + [vmem] * 4,
        out_specs=(hbm, vmem),
        scratch_shapes=scratch,
        compiler_params=pltpu.CompilerParams(
            collective_id=0, has_side_effects=True, vmem_limit_bytes=63 * 1024 * 1024
        ),
        cost_estimate=pl.CostEstimate(
            flops=12_000_000_000, bytes_accessed=25_000_000, transcendentals=600_000
        ),
    )(
        exp_hidden, exp_pre_gain.reshape(1, KDIM), exp_gate, exp_up, exp_down,
        exp_out_gain.reshape(1, KDIM), exp_head.reshape(16, KDIM, WIDE), ama_hidden, ama_out_gain.reshape(1, KAMA),
        ama_head, logit_scale.reshape(4, 128), prompt_of.reshape(1, ROWS), prior_picks,
        valid_mask.reshape(1, WIDE),
    )
    scores, best = pl.pallas_call(
        finish,
        out_shape=(
            jax.ShapeDtypeStruct((ROWS, WIDE), F32),
            jax.ShapeDtypeStruct((1, ROWS), F32),
        ),
        in_specs=[vmem] * 3,
        out_specs=(vmem, vmem),
    )(raw, stats, valid_mask.reshape(1, WIDE))
    return scores, best.reshape(ROWS)


def solution(mesh):
    torus = Mesh(mesh.devices.reshape(4, 2, 4, 2, 2), AXES)
    in_specs = (
        P(REP, TP), P(TP), P(TP, REP), P(TP, REP), P(REP, TP), P(TP), P(None, ALL),
        P(REP, TP), P(TP), P(None, ALL), P(), P(), P(), P(ALL),
    )
    out_specs = (P(None, ALL), P())
    return jax.shard_map(body, mesh=torus, in_specs=in_specs, out_specs=out_specs, check_vma=False)
```

time: 210 us -> 172 us (0.82)
  Pallas kernels: 205 us -> 171 us
  local copies, waits for them, and re-layouts: 3.52 us -> 0 us
    pallas_call x1, Pallas kernels: 205 us -> 169 us  [body(): pl.pallas_call(kernel, out_shape=(jax.ShapeDtypeStruct((ROWS, WIDE), F32)...]
    unnamed x2 -> x0, local copies, waits for them, and re-layouts: 3.52 us -> none
    pallas_call x0 -> x1, Pallas kernels: none -> 2.45 us  [body(): pl.pallas_call(finish, out_shape=(jax.ShapeDtypeStruct((ROWS, WIDE), F32)...]
where the time goes in v2:
time: 172 us
  Pallas kernels  171 us (99%)
    pallas_call x1, Pallas kernels, body(): pl.pallas_call(kernel, out_shape=(jax.ShapeDtypeStruct((ROWS, WIDE), F32)...  169 us

profile of v2, /device:TPU:0, one launch (start us, length us, event | category | flops | bytes accessed | tf_op | source)
XLA Modules:
  0.0 171.8 jit_solution(5421822868467456587)
XLA Ops:
  0.6 168.7 %shard_map.149 = (f32[512,512]{1,0:T(8,128)}, f32[8,512]{1,0:T(8,128)}) custom-call(bf16[64,512]{1,0:T(8,128)(2,1)} %hid_in.1, f32[1,512]{1,0:T(1,128)} %bitcast.11, bf16[512,3584]{1,0:T(8,128)(2,1)} %gate.1, bf16[512,3584]{1,0:T(8,128)(2,1)} %up.1, bf16[3584,512]{1,0:T(8,128)(2,1)} %down.1, f32[1,512]{1,0:T(1,128)} %bitcast.12, ...), custom_call_target="tpu_custom_call" | custom-call | flops 12000000000 | bytes 25000000 | tf_op jit(solution)/shard_map/pallas_call | solution.py:665
  169.4 2.5 %shard_map.150 = (f32[512,512]{1,0:T(8,128)}, f32[1,512]{1,0:T(1,128)}) custom-call(f32[512,512]{1,0:T(8,128)} %get-tuple-element.6.raw, f32[8,512]{1,0:T(8,128)} %get-tuple-element.7.stats, s32[1,512]{1,0:T(1,128)} %bitcast.9), custom_call_target="tpu_custom_call" | custom-call | tf_op jit(solution)/shard_map/pallas_call | solution.py:686

commit v3 on v2

--- a/solution.py
+++ b/solution.py
@@ -26,6 +26,8 @@
 HALF = 1792
 CHUNK = 256
 CHUNKS = HALF // CHUNK
+XFIRST = 4
+YFIRST = CHUNKS - XFIRST
 KAMA = 256
 WIDE = 512
 BF16 = jnp.bfloat16
@@ -62,7 +64,7 @@
     hid_in, pre_gain, gate, up, down, out_gain, head, ama_in, ama_gain, ahead,
     lscale, prompt, picks, valid,
     raw_out, stats_out,
-    XR, XG, W, DOWN, HEADA, HEADB, AHEAD, PB, RR, HID, ACC, OB, OR, FE, FA, AIN, LE, LA,
+    XR, XG, W, DOWN, HEADA, HEADB, AHEAD, PB, M1, SR, T, HS, HR, YR, HID, ACC, OB, OR, FE, FA, AIN, LE, LA,
     STS, ST, FS, FR, SFS, SF, SGS, SG, RE, CNT, SBUF, PG, OG, AG,
     s_loc, s_wl, s_ws, s_wr, s_xs, s_xr, s_bs, s_br, s_sts, s_str, s_frs, s_frr,
     s_rs, s_rr, s_hs, s_hr, s_cs, s_cr, s_os, s_or, s_rings, s_ringr, s_fs, s_fr,
@@ -74,6 +76,7 @@
     b = x * 2 + h
     t = x * 4 + h * 2 + c
     y = h * 2 + l
+    xp, xn, xo = lax.rem(x + 3, 4), lax.rem(x + 1, 4), lax.rem(x + 2, 4)
 
     def remote(src, dst, ss, rs, **where):
         return pltpu.make_async_remote_copy(
@@ -87,6 +90,15 @@
         cp = remote(src, dst, ss, rs, **where)
         cp.start()
         sends.append(cp)
+
+    later = []
+
+    def send_set(region, ss, rs, where):
+        remote(region(), region(), ss, rs, **where()).start()
+        later.append(lambda: remote(region(), region(), ss, rs, **where()).wait_send())
+
+    def go(src, dst, ss, rs, **where):
+        remote(src, dst, ss, rs, **where).start()
 
     def recv(dst, rs):
         remote(dst, dst, rs, rs, c=sib).wait_recv()
@@ -125,7 +137,7 @@
     ]
     for cp in first:
         cp.start()
-    for j in range(CHUNKS):
+    for j in (0, 4, 1, 5, 2, 6, 3):
         wlocal(j, 0, gate).start()
         wlocal(j, 1, up).start()
     late = [
@@ -152,7 +164,7 @@
     for d in range(7):
         pz, q = zl(d, 1)
         send(hid_in, XR.at[r], s_xs.at[d], s_xr.at[d], z=pz, l=q)
-    for j in range(CHUNKS):
+    for j in (0, 4, 1, 5, 2, 6, 3):
         for i, ref in enumerate((gate, up)):
             send(
                 ref.at[:, wcols(sib, j)], wpart(j, c, i),
@@ -165,20 +177,22 @@
         lo, hi = pl.ds(0, 32), pl.ds(32, 32)
         full = pl.ds(0, 64)
 
+        def pass_on(p, rows, q, n):
+            send_set(
+                lambda: sets(p, rows), s_rings.at[index, n], s_ringr.at[index, n], lambda: places(q)
+            )
+
         def start():
-            mine = sets(me, full)
-            send(mine, mine, s_rings.at[index, 0], s_ringr.at[index, 0], **places(nxt))
-            send(mine, mine, s_rings.at[index, 1], s_ringr.at[index, 1], **places(prv))
+            pass_on(me, full, nxt, 0)
+            pass_on(me, full, prv, 1)
 
         def pass_next():
             recv(sets(prv, full), s_ringr.at[index, 0])
-            part = sets(prv, lo)
-            send(part, part, s_rings.at[index, 2], s_ringr.at[index, 2], **places(nxt))
+            pass_on(prv, lo, nxt, 2)
 
         def pass_prev():
             recv(sets(nxt, full), s_ringr.at[index, 1])
-            part = sets(nxt, hi)
-            send(part, part, s_rings.at[index, 3], s_ringr.at[index, 3], **places(prv))
+            pass_on(nxt, hi, prv, 3)
 
         def finish():
             recv(sets(opp, lo), s_ringr.at[index, 2])
@@ -187,7 +201,7 @@
         return start, pass_next, pass_prev, finish, (me, prv, nxt, opp)
 
     def y_place(p):
-        return dict(h=p // 2, l=lax.rem(p, 2))
+        return dict(h=lax.div(p, 2), l=lax.rem(p, 2))
 
     every4, every2 = pl.ds(0, 4), pl.ds(0, 2)
 
@@ -195,13 +209,13 @@
         a = ring(first_index, lambda p, k: ref.at[p, h, c, z, l, k, cols], lambda p: dict(x=p), x)
         bb = ring(
             first_index + 1,
-            lambda p, k: ref.at[every4, p // 2, c, z, lax.rem(p, 2), k, cols], y_place, y,
+            lambda p, k: ref.at[every4, lax.div(p, 2), c, z, lax.rem(p, 2), k, cols], y_place, y,
         )
         if split:
             def d(yy, n):
                 return ring(
                     first_index + 6 + n,
-                    lambda p, k: ref.at[every4, yy // 2, c, p, lax.rem(yy, 2), k, cols],
+                    lambda p, k: ref.at[every4, lax.div(yy, 2), c, p, lax.rem(yy, 2), k, cols],
                     lambda p: dict(z=p), z,
                 )
         else:
@@ -215,13 +229,13 @@
         a = ring(first_index, lambda p, k: ref.at[x, h, c, p, l, k, cols], lambda p: dict(z=p), z)
         bb = ring(
             first_index + 1,
-            lambda p, k: ref.at[x, p // 2, c, every4, lax.rem(p, 2), k, cols], y_place, y,
+            lambda p, k: ref.at[x, lax.div(p, 2), c, every4, lax.rem(p, 2), k, cols], y_place, y,
         )
 
         def d(yy, n):
             return ring(
                 first_index + 6 + n,
-                lambda p, k: ref.at[p, yy // 2, c, every4, lax.rem(yy, 2), k, cols],
+                lambda p, k: ref.at[p, lax.div(yy, 2), c, every4, lax.rem(yy, 2), k, cols],
                 lambda p: dict(x=p), x,
             )
 
@@ -234,8 +248,9 @@
         return ref.at[p, every2, cc, every4, every2, pl.ds(0, 64), cols]
 
     def to_core(ref, maker, p, cols, index, n):
-        s = maker(ref, c, p, cols)
-        send(s, s, s_fs.at[index, n], s_fr.at[index, n], c=sib)
+        send_set(
+            lambda: maker(ref, c, p, cols), s_fs.at[index, n], s_fr.at[index, n], lambda: dict(c=sib)
+        )
 
     def from_other(ref, maker, p, cols, index, n):
         recv(maker(ref, sib, p, cols), s_fr.at[index, n])
@@ -289,29 +304,50 @@
         recv(XG.at[sib, pz * 2 + q], s_br.at[d])
     recv(XG.at[sib, r], s_br.at[7])
 
-    def rs_copy(j, d):
-        px, ph = xh(d, 1)
-        rows = pl.ds(aligned((px * 2 + ph) * BLOCK, BLOCK), BLOCK)
-        return remote(PB.at[j, rows, :], RR.at[j, d], s_rs.at[j], s_rr.at[j], x=px, h=ph)
-
-    def products(j, _):
+    gates, ups = pl.ds(0, CHUNK), pl.ds(CHUNK, CHUNK)
+
+    def piece(j, p, cols, xfirst):
+        return PB.at[j, p, :, :, cols] if xfirst else YR.at[j - XFIRST, p, :, cols]
+
+    def slot(ref, j, n, xfirst):
+        return ref.at[j, n] if xfirst else ref.at[j, n, 0]
+
+    def slots(ref, j, xfirst):
+        return ref.at[j] if xfirst else ref.at[j, :, 0]
+
+    def first_sends(j, xfirst):
+        for p, cols, ref, n, k, to in (
+            (xo, gates, M1, 0, 0, xn), (xo, ups, M1, 1, 0, xp),
+            (xn, ups, SR, 0, 1, xn), (xp, gates, SR, 1, 1, xp),
+        ):
+            go(piece(j, p, cols, xfirst), slot(ref, j, n, xfirst), s_rs.at[j, 0], s_rr.at[j, k], x=to)
+
+    def product(j):
         for i, ref in enumerate((gate, up)):
             wlocal(j, i, ref).wait()
             recv(wpart(j, sib, i), s_wr.at[j, i])
 
         def block(q, _):
-            rows = pl.ds(aligned(q * 256, 256), 256)
             quad = pl.ds(q * 4, 4)
             lhs = jnp.concatenate([XG[k, quad].reshape(256, KDIM) for k in range(2)], axis=1)
-            PB[j, rows, :] = dot(lhs, W[j]).astype(BF16)
+            PB[j, pl.ds(q * 2, 2)] = dot(lhs, W[j]).astype(BF16).reshape(2, 2, BLOCK, 2 * CHUNK)
             return 0
 
         lax.fori_loop(0, 2, block, 0)
-        for d in range(7):
-            rs_copy(j, d).start()
+
+    def products(i, _):
+        product(i)
+        first_sends(i, True)
+
+        @pl.when(i < YFIRST)
+        def _():
+            j = i + XFIRST
+            product(j)
+            go(PB.at[j, :, 1 - h], YR.at[i], s_rs.at[j, 2], s_rr.at[j, 2], h=1 - h)
+
         return 0
 
-    lax.fori_loop(0, CHUNKS, products, 0)
+    lax.fori_loop(0, XFIRST, products, 0)
 
     ama[0][3]()
     ama[1][0]()
@@ -331,35 +367,134 @@
     ama[1][3]()
     ama[2][0]()
 
-    own_rows = pl.ds(aligned(b * BLOCK, BLOCK), BLOCK)
-
-    def hid_copy(j, d):
-        px, ph = xh(d, 1)
-        piece = HID.at[c, j, own_rows, :]
-        return remote(piece, piece, s_hs.at[j], s_hr.at[j], x=px, h=ph)
-
-    def hidden(j, _):
-        recv(RR.at[j], s_rr.at[j])
-        both = PB[j, own_rows, :].astype(F32)
-        for d in range(7):
-            both += RR[j, d].astype(F32)
-        g = both[:, :CHUNK]
-        u = both[:, CHUNK:]
-        HID[c, j, own_rows, :] = (g / (1.0 + jnp.exp(-g)) * u).astype(BF16)
-        for d in range(7):
-            hid_copy(j, d).start()
+    def add_and_pass(j, xfirst):
+        recv(slots(M1, j, xfirst), s_rr.at[j, 0])
+        for n, p, cols in ((0, xn, gates), (1, xp, ups)):
+            ref = slot(M1, j, n, xfirst)
+            ref[...] = (ref[...].astype(F32) + piece(j, p, cols, xfirst)[...].astype(F32)).astype(BF16)
+            go(ref, slot(SR, j, n + 2, xfirst), s_rs.at[j, 1], s_rr.at[j, 1], x=p)
+
+    def ring_sums(j, xfirst):
+        recv(slots(SR, j, xfirst), s_rr.at[j, 1])
+        terms = [slot(SR, j, n, xfirst)[...].astype(F32) for n in range(4)]
+        g = piece(j, x, gates, xfirst)[...].astype(F32) + terms[1] + terms[2]
+        u = piece(j, x, ups, xfirst)[...].astype(F32) + terms[0] + terms[3]
+        return g, u
+
+    def put_hidden(j, g, u):
+        HID[c, j, x, h] = (g / (1.0 + jnp.exp(-g)) * u).astype(BF16)
+
+    def around(j, own):
+        go(own, own, s_hs.at[j, 1], s_hr.at[j, 1], x=xn)
+        go(own, own, s_hs.at[j, 1], s_hr.at[j, 2], x=xp)
+
+    def halves_on(j, blocks):
+        for p, q, n, first_row in ((xp, xn, 1, 0), (xn, xp, 2, 32)):
+            recv(blocks(p, pl.ds(0, BLOCK)), s_hr.at[j, n])
+            part = blocks(p, pl.ds(first_row, 32))
+            go(part, part, s_hs.at[j, 2], s_hr.at[j, 3], x=q)
+
+    def core_copy(j):
+        return remote(HID.at[c, j], HID.at[c, j], s_cs.at[j], s_cr.at[j], c=sib)
+
+    def use_chunk(j):
+        recv(HID.at[sib, j], s_cr.at[j])
+
+        def block(q, _):
+            rows = pl.ds(aligned(q * 256, 256), 256)
+            pair = pl.ds(q * 2, 2)
+            lhs = jnp.concatenate([HID[k, j, pair].reshape(256, CHUNK) for k in range(2)], axis=1)
+            rhs = jnp.concatenate(
+                [DOWN[pl.ds(aligned(k * HALF + j * CHUNK, CHUNK), CHUNK), :] for k in range(2)], axis=0
+            )
+            ACC[rows, :] += dot(lhs, rhs)
+            return 0
+
+        lax.fori_loop(0, 2, block, 0)
+
+    def x0(j):
+        add_and_pass(j, True)
+
+    def x1(j):
+        g, u = ring_sums(j, True)
+        T[j, :, :, gates] = g
+        T[j, :, :, ups] = u
+        HS[j] = T[j, 1 - h].astype(BF16)
+        go(HS.at[j], HR.at[j], s_rs.at[j, 2], s_rr.at[j, 2], h=1 - h)
+
+    def x2(j):
+        recv(HR.at[j], s_rr.at[j, 2])
+        both = T[j, h] + HR[j].astype(F32)
+        put_hidden(j, both[:, :CHUNK], both[:, CHUNK:])
+        own = HID.at[c, j, x, h]
+        go(own, own, s_hs.at[j, 0], s_hr.at[j, 0], h=1 - h)
+
+    def x3(j):
+        recv(HID.at[c, j, x, 1 - h], s_hr.at[j, 0])
+        around(j, HID.at[c, j, x])
+
+    def x4(j):
+        halves_on(j, lambda p, rows: HID.at[c, j, p, :, rows])
+
+    def x5(j):
+        recv(HID.at[c, j, xo], s_hr.at[j, 3])
+        core_copy(j).start()
+
+    def y0(i):
+        j = i + XFIRST
+        recv(YR.at[i], s_rr.at[j, 2])
+        YR[i] = (YR[i].astype(F32) + PB[j, :, h].astype(F32)).astype(BF16)
+        first_sends(j, False)
+
+    def y1(i):
+        add_and_pass(i + XFIRST, False)
+
+    def y2(i):
+        j = i + XFIRST
+        g, u = ring_sums(j, False)
+        put_hidden(j, g, u)
+        around(j, HID.at[c, j, x, h])
+
+    def y3(i):
+        j = i + XFIRST
+        halves_on(j, lambda p, rows: HID.at[c, j, p, h, rows])
+
+    def y4(i):
+        j = i + XFIRST
+        recv(HID.at[c, j, xo, h], s_hr.at[j, 3])
+        got = HID.at[c, j, :, h]
+        go(got, got, s_hs.at[j, 0], s_hr.at[j, 0], h=1 - h)
+
+    def y5(i):
+        j = i + XFIRST
+        recv(HID.at[c, j, :, 1 - h], s_hr.at[j, 0])
+        core_copy(j).start()
+
+    def y6(i):
+        use_chunk(i + XFIRST)
+
+    xstages = (x0, x1, x2, x3, x4, x5, use_chunk)
+    ystages = (y0, y1, y2, y3, y4, y5, y6)
+    ACC[...] = jnp.zeros_like(ACC)
+    late[0].wait()
+    a_places = ama[2][4]
+    ama_cols = pl.ds(0, KAMA)
+
+    def stages(n, _):
+        for k in reversed(range(7)):
+            for many, steps in ((YFIRST, ystages), (XFIRST, xstages)):
+                pl.when((n - k >= 0) & (n - k < many))(functools.partial(steps[k], n - k))
+
         return 0
 
-    lax.fori_loop(0, 3, hidden, 0)
+    lax.fori_loop(0, 5, stages, 0)
     ama[2][1]()
     ama[2][2]()
-    lax.fori_loop(3, 5, hidden, 0)
+    lax.fori_loop(5, 8, stages, 0)
     ama[2][3]()
-    a_places = ama[2][4]
-    ama_cols = pl.ds(0, KAMA)
-    for n in range(4):
-        to_core(FA, a_set, a_places[n], ama_cols, 0, n)
-    lax.fori_loop(5, CHUNKS, hidden, 0)
+    for k in range(4):
+        to_core(FA, a_set, a_places[k], ama_cols, 0, k)
+    lax.fori_loop(8, XFIRST + 6, stages, 0)
 
     late[1].wait()
     for n in range(4):
@@ -380,46 +515,6 @@
         return 0
 
     lax.fori_loop(0, 2, ama_block, 0)
-
-    late[0].wait()
-    ACC[...] = jnp.zeros_like(ACC)
-
-    def core_copy(j):
-        return remote(HID.at[c, j], HID.at[c, j], s_cs.at[j], s_cr.at[j], c=sib)
-
-    def gathered(j, _):
-        recv(HID.at[c, j, pl.ds(0, 7 * BLOCK), :], s_hr.at[j])
-        core_copy(j).start()
-
-        def block(q, _):
-            rows = pl.ds(aligned(q * 256, 256), 256)
-            depth = pl.ds(aligned(c * HALF + j * CHUNK, CHUNK), CHUNK)
-            ACC[rows, :] += dot(HID[c, j, rows, :], DOWN[depth, :])
-            return 0
-
-        lax.fori_loop(0, 2, block, 0)
-        return 0
-
-    def from_core(j, _):
-        recv(HID.at[sib, j], s_cr.at[j])
-
-        def block(q, _):
-            rows = pl.ds(aligned(q * 256, 256), 256)
-            depth = pl.ds(aligned(sib * HALF + j * CHUNK, CHUNK), CHUNK)
-            ACC[rows, :] += dot(HID[sib, j, rows, :], DOWN[depth, :])
-            return 0
-
-        lax.fori_loop(0, 2, block, 0)
-        return 0
-
-    def step(j, _):
-        gathered(j, 0)
-        from_core(j - 1, 0)
-        return 0
-
-    gathered(0, 0)
-    lax.fori_loop(1, CHUNKS, step, 0)
-    from_core(CHUNKS - 1, 0)
 
     for q in range(8):
         OB[q] = ACC[q * BLOCK : (q + 1) * BLOCK, :].astype(BF16)
@@ -590,12 +685,31 @@
 
     for cp in sends:
         cp.wait_send()
+    for wait in later:
+        wait()
 
     def drain(j, _):
-        sent = RR.at[j]
-        remote(sent, sent, s_rs.at[j], s_rr.at[j], c=sib).wait_send()
-        sent = HID.at[c, j, pl.ds(0, 7 * BLOCK), :]
-        remote(sent, sent, s_hs.at[j], s_hr.at[j], c=sib).wait_send()
+        def sent(region, sem):
+            remote(region, region, sem, sem, c=sib).wait_send()
+
+        @pl.when(j < XFIRST)
+        def _():
+            sent(SR.at[j], s_rs.at[j, 0])
+            sent(M1.at[j], s_rs.at[j, 1])
+            sent(HR.at[j], s_rs.at[j, 2])
+            sent(HID.at[c, j, x, h], s_hs.at[j, 0])
+            sent(HID.at[c, j, pl.ds(0, 2)], s_hs.at[j, 1])
+            sent(HID.at[c, j, x], s_hs.at[j, 2])
+
+        @pl.when(j >= XFIRST)
+        def _():
+            sent(SR.at[j, :, 0], s_rs.at[j, 0])
+            sent(M1.at[j, :, 0], s_rs.at[j, 1])
+            sent(YR.at[j - XFIRST], s_rs.at[j, 2])
+            sent(HID.at[c, j, :, h], s_hs.at[j, 0])
+            sent(HID.at[c, j, x], s_hs.at[j, 1])
+            sent(HID.at[c, j, x, h], s_hs.at[j, 2])
+
         core_copy(j).wait_send()
         return 0
 
@@ -630,9 +744,14 @@
         pltpu.VMEM((16, 256, WIDE), BF16),
         pltpu.VMEM((16, 256, WIDE), BF16),
         pltpu.VMEM((DA, WIDE), BF16),
-        pltpu.VMEM((CHUNKS, ROWS, 2 * CHUNK), BF16),
-        pltpu.VMEM((CHUNKS, 7, BLOCK, 2 * CHUNK), BF16),
-        pltpu.VMEM((2, CHUNKS, ROWS, CHUNK), BF16),
+        pltpu.VMEM((CHUNKS, 4, 2, BLOCK, 2 * CHUNK), BF16),
+        pltpu.VMEM((CHUNKS, 2, 2, BLOCK, CHUNK), BF16),
+        pltpu.VMEM((CHUNKS, 4, 2, BLOCK, CHUNK), BF16),
+        pltpu.VMEM((XFIRST, 2, BLOCK, 2 * CHUNK), F32),
+        pltpu.VMEM((XFIRST, BLOCK, 2 * CHUNK), BF16),
+        pltpu.VMEM((XFIRST, BLOCK, 2 * CHUNK), BF16),
+        pltpu.VMEM((YFIRST, 4, BLOCK, 2 * CHUNK), BF16),
+        pltpu.VMEM((2, CHUNKS, 4, 2, BLOCK, CHUNK), BF16),
         pltpu.VMEM((ROWS, KDIM), F32),
         pltpu.VMEM((8, BLOCK, KDIM), BF16),
         pltpu.VMEM((7, BLOCK, KDIM), BF16),
@@ -657,7 +776,7 @@
         pltpu.VMEM((1, KAMA), F32),
         dma((9,)), dma((CHUNKS, 2)), dma((CHUNKS, 2)), dma((CHUNKS, 2)),
         dma((7,)), dma((7,)), dma((8,)), dma((8,)), dma((15,)), dma((1,)), dma((7,)), dma((1,)),
-        dma((CHUNKS,)), dma((CHUNKS,)), dma((CHUNKS,)), dma((CHUNKS,)),
+        dma((CHUNKS, 3)), dma((CHUNKS, 3)), dma((CHUNKS, 3)), dma((CHUNKS, 4)),
         dma((CHUNKS,)), dma((CHUNKS,)), dma((7,)), dma((1,)),
         dma((17, 4)), dma((17, 4)), dma((3, 4)), dma((3, 4)),
         dma((15,)), dma((1,)), dma((7,)), dma((1,)), dma((4, 4)), dma((4, 4)), dma((4,)),

time: 172 us -> 159 us (0.924)
  Pallas kernels: 171 us -> 158 us
    pallas_call x1, Pallas kernels: 169 us -> 156 us  [body(): pl.pallas_call(kernel, out_shape=(jax.ShapeDtypeStruct((ROWS, WIDE), F32)...]
where the time goes in v3:
time: 159 us
  Pallas kernels  158 us (99%)
    pallas_call x1, Pallas kernels, body(): pl.pallas_call(kernel, out_shape=(jax.ShapeDtypeStruct((ROWS, WIDE), F32)...  156 us

profile of v3, /device:TPU:0, one launch (start us, length us, event | category | flops | bytes accessed | tf_op | source)
XLA Modules:
  0.0 158.9 jit_solution(14446115514216007100)
XLA Ops:
  0.6 155.8 %shard_map.149 = (f32[512,512]{1,0:T(8,128)}, f32[8,512]{1,0:T(8,128)}) custom-call(bf16[64,512]{1,0:T(8,128)(2,1)} %hid_in.1, f32[1,512]{1,0:T(1,128)} %bitcast.11, bf16[512,3584]{1,0:T(8,128)(2,1)} %gate.1, bf16[512,3584]{1,0:T(8,128)(2,1)} %up.1, bf16[3584,512]{1,0:T(8,128)(2,1)} %down.1, f32[1,512]{1,0:T(1,128)} %bitcast.12, ...), custom_call_target="tpu_custom_call" | custom-call | flops 12000000000 | bytes 25000000 | tf_op jit(solution)/shard_map/pallas_call | solution.py:784
  156.4 2.5 %shard_map.150 = (f32[512,512]{1,0:T(8,128)}, f32[1,512]{1,0:T(1,128)}) custom-call(f32[512,512]{1,0:T(8,128)} %get-tuple-element.6.raw, f32[8,512]{1,0:T(8,128)} %get-tuple-element.7.stats, s32[1,512]{1,0:T(1,128)} %bitcast.9), custom_call_target="tpu_custom_call" | custom-call | tf_op jit(solution)/shard_map/pallas_call | solution.py:805

commit v4 on v3

--- a/solution.py
+++ b/solution.py
@@ -199,6 +199,25 @@
             recv(sets(opp, hi), s_ringr.at[index, 3])
 
         return start, pass_next, pass_prev, finish, (me, prv, nxt, opp)
+
+    def spread(index, sets, places, me):
+        full = pl.ds(0, 64)
+
+        def to(d):
+            send_set(
+                lambda: sets(me, full), s_rings.at[index, d], s_ringr.at[index, d],
+                lambda: places(lax.rem(me + d, 4)),
+            )
+
+        def start():
+            for d in (1, 3, 2):
+                to(d)
+
+        def finish():
+            for d in (1, 3, 2):
+                recv(sets(lax.rem(me + 4 - d, 4), full), s_ringr.at[index, d])
+
+        return start, finish
 
     def y_place(p):
         return dict(h=lax.div(p, 2), l=lax.rem(p, 2))
@@ -279,8 +298,15 @@
     own_factors = to_column(FS[0:1, :])
 
     FA[x, h, c, z, l] = (values_a * own_factors[BLOCK:] * AG[...]).astype(BF16)
-    ama = rings_x_y_z(FA, pl.ds(0, KAMA), 0)
-    ama[0][0]()
+    ama_cols = pl.ds(0, KAMA)
+    ama = rings_x_y_z(FA, ama_cols, 0)
+    ama_x = spread(
+        0, lambda p, k: FA.at[p, h, c, z, l, k, ama_cols], lambda p: dict(x=p), x
+    )
+    ama_y = spread(
+        1, lambda p, k: FA.at[every4, lax.div(p, 2), c, z, lax.rem(p, 2), k, ama_cols], y_place, y
+    )
+    ama_x[0]()
 
     def take_rows(rr, d, factors):
         XG[c, rr] = (XR[rr].astype(F32) * factors[:BLOCK] * PG[...]).astype(BF16)
@@ -296,8 +322,8 @@
         recv(XR.at[rr], s_xr.at[d])
         take_rows(rr, d, to_column(FR[d, 0:1, :]))
 
-    ama[0][1]()
-    ama[0][2]()
+    ama_x[1]()
+    ama_y[0]()
 
     for d in range(7):
         pz, q = zl(d, -1)
@@ -349,8 +375,6 @@
 
     lax.fori_loop(0, XFIRST, products, 0)
 
-    ama[0][3]()
-    ama[1][0]()
 
     ids = t * WIDE + r * (16 * WIDE) + lax.broadcasted_iota(jnp.int32, (16, WIDE), 1)
     per_prompt = jnp.zeros((16, WIDE), F32)
@@ -362,9 +386,7 @@
         preferred_element_type=F32,
     )
 
-    ama[1][1]()
-    ama[1][2]()
-    ama[1][3]()
+    ama_y[1]()
     ama[2][0]()
 
     def add_and_pass(j, xfirst):
@@ -478,7 +500,6 @@
     ACC[...] = jnp.zeros_like(ACC)
     late[0].wait()
     a_places = ama[2][4]
-    ama_cols = pl.ds(0, KAMA)
 
     def stages(n, _):
         for k in reversed(range(7)):
@@ -496,6 +517,12 @@
         to_core(FA, a_set, a_places[k], ama_cols, 0, k)
     lax.fori_loop(8, XFIRST + 6, stages, 0)
 
+    for q in range(8):
+        OB[q] = ACC[q * BLOCK : (q + 1) * BLOCK, :].astype(BF16)
+    for d in range(7):
+        pz, q = zl(d, 1)
+        send(OB.at[pz * 2 + q], OR.at[d], s_os.at[d], s_or.at[0], z=pz, l=q)
+
     late[1].wait()
     for n in range(4):
         from_other(FA, a_set, a_places[n], ama_cols, 0, n)
@@ -516,11 +543,6 @@
 
     lax.fori_loop(0, 2, ama_block, 0)
 
-    for q in range(8):
-        OB[q] = ACC[q * BLOCK : (q + 1) * BLOCK, :].astype(BF16)
-    for d in range(7):
-        pz, q = zl(d, 1)
-        send(OB.at[pz * 2 + q], OR.at[d], s_os.at[d], s_or.at[0], z=pz, l=q)
     layer = values_x + ACC[pl.ds(aligned(r * BLOCK, BLOCK), BLOCK), :]
     recv(OR, s_or.at[0])
     for d in range(7):
@@ -601,10 +623,15 @@
         for e in (last_one, last_two):
             e[n][1]()
             e[n][2]()
+        if n == 1:
+            from_other(FE, a_set, z, low, 1, 0)
+            use_a(z)
+            from_other(FE, b_set, x, high, 2, 0)
+            use_b(x)
     for n in (1, 2):
         to_core(FE, a_set, za[n], low, 1, n)
         to_core(FE, b_set, xb[n], high, 2, n)
-    for n in range(3):
+    for n in (1, 2):
         from_other(FE, a_set, za[n], low, 1, n)
         use_a(za[n])
         from_other(FE, b_set, xb[n], high, 2, n)

time: 159 us -> 146 us (0.918)
  Pallas kernels: 158 us -> 146 us
    pallas_call x1, Pallas kernels: 156 us -> 143 us  [body(): pl.pallas_call(kernel, out_shape=(jax.ShapeDtypeStruct((ROWS, WIDE), F32)...]
where the time goes in v4:
time: 146 us
  Pallas kernels  146 us (100%)
    pallas_call x1, Pallas kernels, body(): pl.pallas_call(kernel, out_shape=(jax.ShapeDtypeStruct((ROWS, WIDE), F32)...  143 us

profile of v4, /device:TPU:0, one launch (start us, length us, event | category | flops | bytes accessed | tf_op | source)
XLA Modules:
  0.0 146.3 jit_solution(5766773844102276321)
XLA Ops:
  0.6 143.2 %shard_map.149 = (f32[512,512]{1,0:T(8,128)}, f32[8,512]{1,0:T(8,128)}) custom-call(bf16[64,512]{1,0:T(8,128)(2,1)} %hid_in.1, f32[1,512]{1,0:T(1,128)} %bitcast.11, bf16[512,3584]{1,0:T(8,128)(2,1)} %gate.1, bf16[512,3584]{1,0:T(8,128)(2,1)} %up.1, bf16[3584,512]{1,0:T(8,128)(2,1)} %down.1, f32[1,512]{1,0:T(1,128)} %bitcast.12, ...), custom_call_target="tpu_custom_call" | custom-call | flops 12000000000 | bytes 25000000 | tf_op jit(solution)/shard_map/pallas_call | solution.py:811
  143.8 2.5 %shard_map.150 = (f32[512,512]{1,0:T(8,128)}, f32[1,512]{1,0:T(1,128)}) custom-call(f32[512,512]{1,0:T(8,128)} %get-tuple-element.6.raw, f32[8,512]{1,0:T(8,128)} %get-tuple-element.7.stats, s32[1,512]{1,0:T(1,128)} %bitcast.9), custom_call_target="tpu_custom_call" | custom-call | tf_op jit(solution)/shard_map/pallas_call | solution.py:832

commit v5 on v4

--- a/solution.py
+++ b/solution.py
@@ -65,7 +65,7 @@
     lscale, prompt, picks, valid,
     raw_out, stats_out,
     XR, XG, W, DOWN, HEADA, HEADB, AHEAD, PB, M1, SR, T, HS, HR, YR, HID, ACC, OB, OR, FE, FA, AIN, LE, LA,
-    STS, ST, FS, FR, SFS, SF, SGS, SG, RE, CNT, SBUF, PG, OG, AG,
+    STS, ST, FS, FR, SFS, SF, SGS, SG, RE, CNT, SBUF, AST, PG, OG, AG,
     s_loc, s_wl, s_ws, s_wr, s_xs, s_xr, s_bs, s_br, s_sts, s_str, s_frs, s_frr,
     s_rs, s_rr, s_hs, s_hr, s_cs, s_cr, s_os, s_or, s_rings, s_ringr, s_fs, s_fr,
     s_sfs, s_sfr, s_sgs, s_sgr, s_qs, s_qr, s_out,
@@ -159,7 +159,18 @@
         px, ph, pc = tp(d, 1)
         greet(x=px, h=ph, c=pc)
     greet(h=1 - h, l=1 - l)
+    for cp in first:
+        cp.wait()
+    values_x = XR[r].astype(F32)
+    values_a = AIN[...].astype(F32)
+    squares = jnp.concatenate(
+        [jnp.sum(v * v, axis=1, keepdims=True) for v in (values_x, values_a)], axis=0
+    )
+    STS[...] = jnp.broadcast_to(to_row(squares), (8, 128))
     pl.semaphore_wait(barrier, 23)
+    for d in range(15):
+        px, ph, pc = tp(d, 1)
+        send(STS, ST.at[d], s_sts.at[d], s_str.at[0], x=px, h=ph, c=pc)
 
     for d in range(7):
         pz, q = zl(d, 1)
@@ -274,17 +285,6 @@
     def from_other(ref, maker, p, cols, index, n):
         recv(maker(ref, sib, p, cols), s_fr.at[index, n])
 
-    for cp in first:
-        cp.wait()
-    values_x = XR[r].astype(F32)
-    values_a = AIN[...].astype(F32)
-    squares = jnp.concatenate(
-        [jnp.sum(v * v, axis=1, keepdims=True) for v in (values_x, values_a)], axis=0
-    )
-    STS[...] = jnp.broadcast_to(to_row(squares), (8, 128))
-    for d in range(15):
-        px, ph, pc = tp(d, 1)
-        send(STS, ST.at[d], s_sts.at[d], s_str.at[0], x=px, h=ph, c=pc)
     recv(ST, s_str.at[0])
     total = STS[...]
     for d in range(15):
@@ -543,6 +543,20 @@
 
     lax.fori_loop(0, 2, ama_block, 0)
 
+    vmask = valid[...].astype(F32)
+    half_valid = contrast_weight * vmask
+    for q in range(4):
+        rows = pl.ds(q * 128, 128)
+        ls = to_column(lscale[q : q + 1, :])
+        RE[1, rows, :] = jnp.broadcast_to(ls, (128, 128))
+        la = LA[rows, :] * ls
+        ma = jnp.max(la, axis=1, keepdims=True)
+        sa = jnp.sum(jnp.exp(la - ma), axis=1, keepdims=True)
+        AST[0:1, rows] = to_row(ma)
+        AST[1:2, rows] = to_row(sa)
+        LA[rows, :] = half_valid * la + hamming_weight * CNT[rows, :]
+
+
     layer = values_x + ACC[pl.ds(aligned(r * BLOCK, BLOCK), BLOCK), :]
     recv(OR, s_or.at[0])
     for d in range(7):
@@ -552,8 +566,10 @@
     low, high = pl.ds(0, 256), pl.ds(256, 256)
     one = rings_x_y_z(FE, low, 3, split=True)
     two = rings_z_y_x(FE, high, 7)
-    one[0][0]()
-    two[0][0]()
+    one_first = spread(3, lambda p, k: FE.at[p, h, c, z, l, k, low], lambda p: dict(x=p), x)
+    two_first = spread(7, lambda p, k: FE.at[x, h, c, p, l, k, high], lambda p: dict(z=p), z)
+    one_first[0]()
+    two_first[0]()
 
     squares = jnp.sum(layer * layer, axis=1, keepdims=True)
     squares = jnp.concatenate([squares, squares], axis=0)
@@ -562,14 +578,11 @@
         px, ph, pc = tp(d, 1)
         send(SFS, SF.at[d], s_sfs.at[d], s_sfr.at[0], x=px, h=ph, c=pc)
 
-    for g in (one[0], two[0]):
-        g[1]()
-        g[2]()
     y_order = one[1][4]
     last_one = [one[2](p, n) for n, p in enumerate(y_order)]
     last_two = [two[2](p, n) for n, p in enumerate(y_order)]
-    for g, n, e in ((one[0], one[1], last_one), (two[0], two[1], last_two)):
-        g[3]()
+    for g, n, e in ((one_first, one[1], last_one), (two_first, two[1], last_two)):
+        g[1]()
         n[0]()
         e[0][0]()
     for k in (1, 2):
@@ -638,9 +651,6 @@
         use_b(xb[n])
 
     recv(SG, s_sgr.at[0])
-    for q in range(4):
-        ls = to_column(lscale[q : q + 1, :])
-        RE[1, pl.ds(q * 128, 128), :] = jnp.broadcast_to(ls, (128, 128))
 
     def row_factors(rr, line):
         rows = pl.ds(aligned(rr * BLOCK, BLOCK), BLOCK)
@@ -652,34 +662,41 @@
         pz, q = zl(d, -1)
         row_factors(pz * 2 + q, SG[d, 0:1, :])
 
+    def a_group(n):
+        return lambda ref, cc, p, cols: ref.at[
+            every4, lax.div(y_order[n], 2), cc, p, lax.rem(y_order[n], 2), pl.ds(0, 64), cols
+        ]
+
+    def b_group(n):
+        return lambda ref, cc, p, cols: ref.at[
+            p, lax.div(y_order[n], 2), cc, every4, lax.rem(y_order[n], 2), pl.ds(0, 64), cols
+        ]
+
     for n in range(4):
-        for e in (last_one, last_two):
-            e[n][3]()
-    to_core(FE, a_set, za[3], low, 1, 3)
-    to_core(FE, b_set, xb[3], high, 2, 3)
-    from_other(FE, a_set, za[3], low, 1, 3)
+        last_one[n][3]()
+        to_core(FE, a_group(n), za[3], low, 3, n)
+        last_two[n][3]()
+        to_core(FE, b_group(n), xb[3], high, 4, n)
+    for n in range(4):
+        from_other(FE, a_group(n), za[3], low, 3, n)
+        from_other(FE, b_group(n), xb[3], high, 4, n)
     use_a(za[3])
-    from_other(FE, b_set, xb[3], high, 2, 3)
     use_b(xb[3])
 
-    vmask = valid[...].astype(F32)
-    half_valid = contrast_weight * vmask
     for q in range(4):
         rows = pl.ds(q * 128, 128)
         le = LE[rows, :] * RE[0, rows, 0:1]
-        la = LA[rows, :] * RE[1, rows, 0:1]
         me = jnp.max(le, axis=1, keepdims=True)
-        ma = jnp.max(la, axis=1, keepdims=True)
         se = jnp.sum(jnp.exp(le - me), axis=1, keepdims=True)
-        sa = jnp.sum(jnp.exp(la - ma), axis=1, keepdims=True)
-        raw = le - half_valid * la - hamming_weight * CNT[rows, :]
+        raw = le - LA[rows, :]
         LE[rows, :] = raw
         local(LE.at[rows], raw_out.at[rows], s_out.at[q]).start()
         used = jnp.broadcast_to(vmask, raw.shape) > 0.5
         m1 = jnp.max(jnp.where(used, raw, LOWEST), axis=1, keepdims=True)
         m0 = jnp.max(jnp.where(used, LOWEST, raw), axis=1, keepdims=True)
-        lines = [to_row(v) for v in (me, se, ma, sa, m1, m0, me, me)]
-        SBUF[0, c, :, rows] = jnp.concatenate(lines, axis=0)
+        line_e, line_s, line_1, line_0 = (to_row(v) for v in (me, se, m1, m0))
+        lines = [line_e, line_s, AST[0:1, rows], AST[1:2, rows], line_1, line_0, line_e, line_e]
+        SBUF[0, x * 2 + c, :, rows] = jnp.concatenate(lines, axis=0)
 
     def merge(parts):
         me = functools.reduce(jnp.maximum, [p[0:1] for p in parts])
@@ -690,12 +707,18 @@
         m0 = functools.reduce(jnp.maximum, [p[5:6] for p in parts])
         return jnp.concatenate([me, se, ma, sa, m1, m0, me, me], axis=0)
 
-    mine = SBUF.at[0, c]
-    send(mine, mine, s_qs.at[0, 0], s_qr.at[0, 0], c=sib)
-    recv(SBUF.at[0, sib], s_qr.at[0, 0])
-    merged = merge([SBUF[0, 0], SBUF[0, 1]])
+    mine = SBUF.at[0, x * 2 + c]
+    for d in range(1, 8):
+        send(
+            mine, mine, s_qs.at[0, d], s_qr.at[0, d],
+            x=lax.rem(x + d // 2, 4), c=lax.rem(c + d % 2, 2),
+        )
+    for d in range(1, 8):
+        px, pc = lax.rem(x + 4 - d // 2, 4), lax.rem(c + d % 2, 2)
+        recv(SBUF.at[0, px * 2 + pc], s_qr.at[0, d])
+    merged = merge([SBUF[0, k] for k in range(8)])
     for phase, (me, place) in enumerate(
-        ((x, lambda p: dict(x=p)), (y, y_place), (z, lambda p: dict(z=p))), start=1
+        ((y, y_place), (z, lambda p: dict(z=p))), start=1
     ):
         SBUF[phase, me] = merged
         mine = SBUF.at[phase, me]
@@ -797,7 +820,8 @@
         pltpu.VMEM((7, 8, 128), F32),
         pltpu.VMEM((2, ROWS, 128), F32),
         pltpu.VMEM((ROWS, WIDE), F32),
-        pltpu.VMEM((4, 4, 8, ROWS), F32),
+        pltpu.VMEM((3, 8, 8, ROWS), F32),
+        pltpu.VMEM((8, ROWS), F32),
         pltpu.VMEM((1, KDIM), F32),
         pltpu.VMEM((1, KDIM), F32),
         pltpu.VMEM((1, KAMA), F32),
@@ -805,8 +829,8 @@
         dma((7,)), dma((7,)), dma((8,)), dma((8,)), dma((15,)), dma((1,)), dma((7,)), dma((1,)),
         dma((CHUNKS, 3)), dma((CHUNKS, 3)), dma((CHUNKS, 3)), dma((CHUNKS, 4)),
         dma((CHUNKS,)), dma((CHUNKS,)), dma((7,)), dma((1,)),
-        dma((17, 4)), dma((17, 4)), dma((3, 4)), dma((3, 4)),
-        dma((15,)), dma((1,)), dma((7,)), dma((1,)), dma((4, 4)), dma((4, 4)), dma((4,)),
+        dma((17, 4)), dma((17, 4)), dma((5, 4)), dma((5, 4)),
+        dma((15,)), dma((1,)), dma((7,)), dma((1,)), dma((3, 8)), dma((3, 8)), dma((4,)),
     ]
     raw, stats = pl.pallas_call(
         kernel,

time: 146 us -> 144 us (0.986)
  Pallas kernels: 146 us -> 143 us
    pallas_call x1, Pallas kernels: 143 us -> 140 us  [body(): pl.pallas_call(kernel, out_shape=(jax.ShapeDtypeStruct((ROWS, WIDE), F32)...]
where the time goes in v5:
time: 144 us; the launch traced here: 143 us
  Pallas kernels  143 us (99%)
    pallas_call x1, Pallas kernels, body(): pl.pallas_call(kernel, out_shape=(jax.ShapeDtypeStruct((ROWS, WIDE), F32)...  140 us

profile of v5, /device:TPU:0, one launch (start us, length us, event | category | flops | bytes accessed | tf_op | source)
XLA Modules:
  0.0 143.3 jit_solution(2392966395778266291)
XLA Ops:
  0.6 140.3 %shard_map.149 = (f32[512,512]{1,0:T(8,128)}, f32[8,512]{1,0:T(8,128)}) custom-call(bf16[64,512]{1,0:T(8,128)(2,1)} %hid_in.1, f32[1,512]{1,0:T(1,128)} %bitcast.11, bf16[512,3584]{1,0:T(8,128)(2,1)} %gate.1, bf16[512,3584]{1,0:T(8,128)(2,1)} %up.1, bf16[3584,512]{1,0:T(8,128)(2,1)} %down.1, f32[1,512]{1,0:T(1,128)} %bitcast.12, ...), custom_call_target="tpu_custom_call" | custom-call | flops 12000000000 | bytes 25000000 | tf_op jit(solution)/shard_map/pallas_call | solution.py:835
  140.9 2.5 %shard_map.150 = (f32[512,512]{1,0:T(8,128)}, f32[1,512]{1,0:T(1,128)}) custom-call(f32[512,512]{1,0:T(8,128)} %get-tuple-element.6.raw, f32[8,512]{1,0:T(8,128)} %get-tuple-element.7.stats, s32[1,512]{1,0:T(1,128)} %bitcast.9), custom_call_target="tpu_custom_call" | custom-call | tf_op jit(solution)/shard_map/pallas_call | solution.py:856

commit v6 on v5

--- a/solution.py
+++ b/solution.py
@@ -89,13 +89,19 @@
     def send(src, dst, ss, rs, **where):
         cp = remote(src, dst, ss, rs, **where)
         cp.start()
-        sends.append(cp)
+        sends.append(cp.wait_send)
 
     later = []
 
     def send_set(region, ss, rs, where):
         remote(region(), region(), ss, rs, **where()).start()
         later.append(lambda: remote(region(), region(), ss, rs, **where()).wait_send())
+
+    def settle(*lists):
+        for waits in lists:
+            for wait in waits:
+                wait()
+            waits.clear()
 
     def go(src, dst, ss, rs, **where):
         remote(src, dst, ss, rs, **where).start()
@@ -175,12 +181,6 @@
     for d in range(7):
         pz, q = zl(d, 1)
         send(hid_in, XR.at[r], s_xs.at[d], s_xr.at[d], z=pz, l=q)
-    for j in (0, 4, 1, 5, 2, 6, 3):
-        for i, ref in enumerate((gate, up)):
-            send(
-                ref.at[:, wcols(sib, j)], wpart(j, c, i),
-                s_ws.at[j, i], s_wr.at[j, i], c=sib,
-            )
 
     def ring(index, sets, places, me):
         prv, nxt = lax.rem(me + 3, 4), lax.rem(me + 1, 4)
@@ -295,6 +295,12 @@
     for d in range(7):
         pz, q = zl(d, 1)
         send(FS, FR.at[d], s_frs.at[d], s_frr.at[0], z=pz, l=q)
+    for j in (0, 4, 1, 5, 2, 6, 3):
+        for i, ref in enumerate((gate, up)):
+            send(
+                ref.at[:, wcols(sib, j)], wpart(j, c, i),
+                s_ws.at[j, i], s_wr.at[j, i], c=sib,
+            )
     own_factors = to_column(FS[0:1, :])
 
     FA[x, h, c, z, l] = (values_a * own_factors[BLOCK:] * AG[...]).astype(BF16)
@@ -519,9 +525,41 @@
 
     for q in range(8):
         OB[q] = ACC[q * BLOCK : (q + 1) * BLOCK, :].astype(BF16)
+    early = sends + later
+    sends.clear()
+    later.clear()
     for d in range(7):
         pz, q = zl(d, 1)
         send(OB.at[pz * 2 + q], OR.at[d], s_os.at[d], s_or.at[0], z=pz, l=q)
+
+    settle(early)
+
+    def drain(j, _):
+        def sent(region, sem):
+            remote(region, region, sem, sem, c=sib).wait_send()
+
+        @pl.when(j < XFIRST)
+        def _():
+            sent(SR.at[j], s_rs.at[j, 0])
+            sent(M1.at[j], s_rs.at[j, 1])
+            sent(HR.at[j], s_rs.at[j, 2])
+            sent(HID.at[c, j, x, h], s_hs.at[j, 0])
+            sent(HID.at[c, j, pl.ds(0, 2)], s_hs.at[j, 1])
+            sent(HID.at[c, j, x], s_hs.at[j, 2])
+
+        @pl.when(j >= XFIRST)
+        def _():
+            sent(SR.at[j, :, 0], s_rs.at[j, 0])
+            sent(M1.at[j, :, 0], s_rs.at[j, 1])
+            sent(YR.at[j - XFIRST], s_rs.at[j, 2])
+            sent(HID.at[c, j, :, h], s_hs.at[j, 0])
+            sent(HID.at[c, j, x], s_hs.at[j, 1])
+            sent(HID.at[c, j, x, h], s_hs.at[j, 2])
+
+        core_copy(j).wait_send()
+        return 0
+
+    lax.fori_loop(0, CHUNKS, drain, 0)
 
     late[1].wait()
     for n in range(4):
@@ -672,6 +710,7 @@
             p, lax.div(y_order[n], 2), cc, every4, lax.rem(y_order[n], 2), pl.ds(0, 64), cols
         ]
 
+    settle(sends)
     for n in range(4):
         last_one[n][3]()
         to_core(FE, a_group(n), za[3], low, 3, n)
@@ -713,6 +752,7 @@
             mine, mine, s_qs.at[0, d], s_qr.at[0, d],
             x=lax.rem(x + d // 2, 4), c=lax.rem(c + d % 2, 2),
         )
+    settle(later)
     for d in range(1, 8):
         px, pc = lax.rem(x + 4 - d // 2, 4), lax.rem(c + d % 2, 2)
         recv(SBUF.at[0, px * 2 + pc], s_qr.at[0, d])
@@ -733,37 +773,7 @@
         rows = pl.ds(q * 128, 128)
         local(LE.at[rows], raw_out.at[rows], s_out.at[q]).wait()
 
-    for cp in sends:
-        cp.wait_send()
-    for wait in later:
-        wait()
-
-    def drain(j, _):
-        def sent(region, sem):
-            remote(region, region, sem, sem, c=sib).wait_send()
-
-        @pl.when(j < XFIRST)
-        def _():
-            sent(SR.at[j], s_rs.at[j, 0])
-            sent(M1.at[j], s_rs.at[j, 1])
-            sent(HR.at[j], s_rs.at[j, 2])
-            sent(HID.at[c, j, x, h], s_hs.at[j, 0])
-            sent(HID.at[c, j, pl.ds(0, 2)], s_hs.at[j, 1])
-            sent(HID.at[c, j, x], s_hs.at[j, 2])
-
-        @pl.when(j >= XFIRST)
-        def _():
-            sent(SR.at[j, :, 0], s_rs.at[j, 0])
-            sent(M1.at[j, :, 0], s_rs.at[j, 1])
-            sent(YR.at[j - XFIRST], s_rs.at[j, 2])
-            sent(HID.at[c, j, :, h], s_hs.at[j, 0])
-            sent(HID.at[c, j, x], s_hs.at[j, 1])
-            sent(HID.at[c, j, x, h], s_hs.at[j, 2])
-
-        core_copy(j).wait_send()
-        return 0
-
-    lax.fori_loop(0, CHUNKS, drain, 0)
+    settle(sends, later)
 
 
 def finish(raw, stats, valid, scores, best):

time: 144 us -> 143 us (level)
  no operation moved by 1% of the time
where the time goes in v6:
time: 143 us
  Pallas kernels  142 us (99%)
    pallas_call x1, Pallas kernels, body(): pl.pallas_call(kernel, out_shape=(jax.ShapeDtypeStruct((ROWS, WIDE), F32)...  140 us

profile of v6, /device:TPU:0, one launch (start us, length us, event | category | flops | bytes accessed | tf_op | source)
XLA Modules:
  0.0 143.0 jit_solution(5331931365317421505)
XLA Ops:
  0.6 139.9 %shard_map.149 = (f32[512,512]{1,0:T(8,128)}, f32[8,512]{1,0:T(8,128)}) custom-call(bf16[64,512]{1,0:T(8,128)(2,1)} %hid_in.1, f32[1,512]{1,0:T(1,128)} %bitcast.11, bf16[512,3584]{1,0:T(8,128)(2,1)} %gate.1, bf16[512,3584]{1,0:T(8,128)(2,1)} %up.1, bf16[3584,512]{1,0:T(8,128)(2,1)} %down.1, f32[1,512]{1,0:T(1,128)} %bitcast.12, ...), custom_call_target="tpu_custom_call" | custom-call | flops 12000000000 | bytes 25000000 | tf_op jit(solution)/shard_map/pallas_call | solution.py:845
  140.6 2.5 %shard_map.150 = (f32[512,512]{1,0:T(8,128)}, f32[1,512]{1,0:T(1,128)}) custom-call(f32[512,512]{1,0:T(8,128)} %get-tuple-element.6.raw, f32[8,512]{1,0:T(8,128)} %get-tuple-element.7.stats, s32[1,512]{1,0:T(1,128)} %bitcast.9), custom_call_target="tpu_custom_call" | custom-call | tf_op jit(solution)/shard_map/pallas_call | solution.py:866
